TPU v7x, 32 devices: a whole 2x2x4 slice. The times are simulated.
32 devices in a mesh: tok: 4 (over y, x), smp: 8 (over z, core).
Axes of the slice: x: 2, y: 2, z: 4, core: 2. Of those that a mesh axis runs over, the one named last changes fastest.
Arguments:
- row_table: float32 [8, 2048, 384], P('tok', 'smp'), may hold values from -6 to 6
- row_accum: float32 [8, 2048], P('tok', 'smp'), may hold values from 0.0001 to 0.01
- last_step: int32 [8, 2048], P('tok', 'smp'), may hold values from 0 to 47
- step_now: int32 [1], replicated, may hold values from 48 to 63
- row_ids: int32 [8, 8, 8, 2], P('tok', 'smp'), may hold values from 0 to 255, as said below
- row_counts: int32 [8, 8, 8], P('tok', 'smp'), may hold values from 1 to 2, as said below
- sample_slots: int32 [8, 2048], P(None, 'smp'), may hold values from 0 to 15, as said below
- labels: int32 [2048], P('smp'), may hold values 0 or 1
- up_weight: bfloat16 [384, 8, 1536], P('smp', 'tok'), may hold values from -0.3125 to 0.3125
- down_weight: bfloat16 [384, 8, 1536], P('smp', 'tok'), may hold values from -0.15625 to 0.15625
- out_weight: float32 [8, 384], P('tok'), may hold values from -0.3125 to 0.3125
Outputs:
- new_table: float32 [8, 2048, 384], P('tok', 'smp')
- new_accum: float32 [8, 2048], P('tok', 'smp')
- grad_down: float32 [384, 8, 1536], P('smp', 'tok')
- logits: float32 [2048], P('smp')
Inputs may be any that keep to these rules, and one draw needn't show every extreme that they name: The first row_counts[t, o, g] entries of each list are distinct; later entries are padding; every token and owner has a list of 2 valid entries for some group. `row_ids`: row numbers within the owner's shard. `sample_slots`: each slot o * 2 + c names a valid entry c < row_counts[t, o, s // 256]. `last_step`: each row's last step is before step_now.
All inputs are finite; a program needn't handle non-finite values. No bound on the sum of `labels` on one device may be relied on, other than what follows from the above.
Results may differ from a plain program's by a relative error of at most 0.0021.
Values may be sent and summed in bfloat16 or wider, within the bound.
A program may use at most 64 MiB of HBM per device.

v0:
```python
import math

import jax
import jax.numpy as jnp
from jax import lax
from jax.sharding import PartitionSpec as P

decay_log = math.log(0.98)
learn_rate = 0.2
norm_eps = 1e-05


def normalize(values):
    centre = jnp.mean(values, axis=-1, keepdims=True)
    shifted = values - centre
    inverse = lax.rsqrt(jnp.mean(shifted * shifted, axis=-1, keepdims=True) + norm_eps)
    return (shifted * inverse, inverse)


def norm_back(grad_in, normed, inverse):
    first_mean = jnp.mean(grad_in, axis=-1, keepdims=True)
    second = jnp.mean(grad_in * normed, axis=-1, keepdims=True)
    return inverse * (grad_in - first_mean - normed * second)


def gelu_grad(preact):
    cumulative = 0.5 * (1.0 + lax.erf(preact * (1.0 / math.sqrt(2.0))))
    density = jnp.exp(-0.5 * preact * preact) * (1.0 / math.sqrt(2.0 * math.pi))
    return cumulative + preact * density


def on_device(
    row_table,
    row_accum,
    last_step,
    step_now,
    row_ids,
    row_counts,
    sample_slots,
    labels,
    up_weight,
    down_weight,
    out_weight,
):
    highest = lax.Precision.HIGHEST
    local_toks, shard_rows, model_width = row_table.shape
    group_count = row_ids.shape[2]
    capacity = row_ids.shape[3]
    batch_size = labels.shape[0]
    list_len = group_count * capacity
    head_count = sample_slots.shape[0]
    head_width = model_width // head_count
    elapsed = (step_now[0] - last_step).astype(jnp.float32)
    factor = jnp.exp(elapsed * decay_log)
    decayed = row_table * factor[:, :, None]
    owned_ids = row_ids[:, 0].reshape(local_toks, list_len)
    valid_slot = (jnp.arange(capacity)[None, None, :] < row_counts[:, 0][:, :, None]).reshape(
        local_toks, list_len
    )
    looked = jnp.take_along_axis(decayed, owned_ids[:, :, None], axis=1)
    looked = jnp.where(valid_slot[:, :, None], looked, 0.0)
    arrived = lax.all_to_all(
        looked.reshape(local_toks, group_count, capacity, model_width),
        "smp",
        split_axis=1,
        concat_axis=1,
        tiled=True,
    )
    row_lists = arrived.reshape(local_toks, list_len, model_width)
    tok_index = lax.axis_index("tok")
    my_slots = lax.dynamic_slice_in_dim(sample_slots, tok_index * local_toks, local_toks, 0)
    own_rows = jnp.take_along_axis(row_lists, my_slots[:, :, None], axis=1)
    split_lists = row_lists.reshape(local_toks, list_len, head_count, head_width)
    received = lax.all_to_all(split_lists, "tok", split_axis=2, concat_axis=0, tiled=True)
    picked = jnp.take_along_axis(received, sample_slots[:, :, None, None], axis=1)
    mixed_rows = picked.transpose(2, 1, 0, 3).reshape(local_toks, batch_size, model_width)
    normed_in, inverse_in = normalize(own_rows + mixed_rows)
    input_bf = normed_in.astype(jnp.bfloat16)
    up_full, down_full = (
        lax.all_gather(up_weight, "smp", axis=0, tiled=True),
        lax.all_gather(down_weight, "smp", axis=0, tiled=True),
    )
    preact = jnp.einsum("jbd,djf->jbf", input_bf, up_full, preferred_element_type=jnp.float32)
    active = jax.nn.gelu(preact, approximate=False).astype(jnp.bfloat16)
    output = jnp.einsum("jbf,djf->jbd", active, down_full, preferred_element_type=jnp.float32)
    normed_out, inverse_out = normalize(normed_in + output)
    partial_logit = jnp.einsum("jbd,jd->b", normed_out, out_weight, precision=highest)
    logits = lax.psum(partial_logit, "tok")
    dlogit = jax.nn.sigmoid(logits) - labels.astype(jnp.float32)
    grad_norm_out = dlogit[None, :, None] * out_weight[:, None, :]
    grad_sum = norm_back(grad_norm_out, normed_out, inverse_out)
    grad_out_bf = grad_sum.astype(jnp.bfloat16)
    grad_down = lax.psum_scatter(
        jnp.einsum("jbd,jbf->djf", grad_out_bf, active, preferred_element_type=jnp.float32),
        "smp",
        scatter_dimension=0,
        tiled=True,
    )
    grad_active = jnp.einsum(
        "jbd,djf->jbf", grad_out_bf, down_full, preferred_element_type=jnp.float32
    )
    grad_pre = (grad_active * gelu_grad(preact)).astype(jnp.bfloat16)
    grad_normed = grad_sum + jnp.einsum(
        "jbf,djf->jbd", grad_pre, up_full, preferred_element_type=jnp.float32
    )
    grad_mixed = norm_back(grad_normed, normed_in, inverse_in)
    slot_range = jnp.arange(list_len)
    split_grads = grad_mixed.reshape(local_toks, batch_size, head_count, head_width)
    all_hits = (sample_slots[:, None, :] == slot_range[None, :, None]).astype(jnp.float32)
    head_sums = jnp.einsum("tlb,jbte->tlje", all_hits, split_grads, precision=highest)
    returned = lax.all_to_all(head_sums, "tok", split_axis=0, concat_axis=2, tiled=True)
    my_hits = lax.dynamic_slice_in_dim(all_hits, tok_index * local_toks, local_toks, 0)
    list_grads = jnp.einsum(
        "jlb,jbd->jld", my_hits, grad_mixed, precision=highest
    ) + returned.reshape(local_toks, list_len, model_width)
    back_grads = lax.all_to_all(
        list_grads.reshape(local_toks, group_count, capacity, model_width),
        "smp",
        split_axis=1,
        concat_axis=1,
        tiled=True,
    )
    back_grads = back_grads.reshape(local_toks, list_len, model_width)
    row_hits = (
        (owned_ids[:, None, :] == jnp.arange(shard_rows)[None, :, None]) & valid_slot[:, None, :]
    ).astype(jnp.float32)
    row_grads = jnp.einsum("jrk,jkd->jrd", row_hits, back_grads, precision=highest)
    touched = jnp.sum(row_hits, axis=2) > 0.0
    new_accum = row_accum + jnp.mean(row_grads * row_grads, axis=2)
    updated = decayed - learn_rate * row_grads * lax.rsqrt(new_accum)[:, :, None]
    new_table = jnp.where(touched[:, :, None], updated, row_table)
    return (new_table, new_accum, grad_down, logits)


def solution(mesh):
    return jax.shard_map(
        on_device,
        mesh=mesh,
        in_specs=(
            P("tok", "smp", None),
            P("tok", "smp"),
            P("tok", "smp"),
            P(),
            P("tok", "smp", None, None),
            P("tok", "smp", None),
            P(None, "smp"),
            P("smp"),
            P("smp", "tok", None),
            P("smp", "tok", None),
            P("tok", None),
        ),
        out_specs=(P("tok", "smp", None), P("tok", "smp"), P("smp", "tok", None), P("smp")),
        check_vma=False,
    )
```

profile of v0, /device:TPU:0, one launch (start us, length us, event | category | flops | bytes accessed | tf_op | source)
XLA Modules:
  0.0 217.1 jit_solution(8678717273503277775)
XLA Ops:
  7.2 1.8 copy.91
  9.7 0.8 copy.75
  11.3 1.3 broadcast_multiply_fusion
  15.6 6.3 %all-to-all-start = ((f32[2,8,2,384]{3,2,0,1:T(2,128)}), f32[2,8,2,384]{3,2,0,1:T(2,128)S(1)}, u32[]{:S(2)}, u32[]{:S(2)}) async-start(f32[2,8,2,384]{3,2,0,1:T(2,128)} %fusion.31), calls=%async_computation | async-start | bytes 98304 | tf_op jit(solution)/shard_map/all_to_all | solution.py:62
  23.1 5.4 %all-to-all-done = f32[2,8,2,384]{3,2,0,1:T(2,128)S(1)} async-done(((f32[2,8,2,384]{3,2,0,1:T(2,128)}), f32[2,8,2,384]{3,2,0,1:T(2,128)S(1)}, u32[]{:S(2)}, u32[]{:S(2)}) %all-to-all-start) | async-done | bytes 49184 | tf_op jit(solution)/shard_map/all_to_all | solution.py:62
  28.7 0.8 reshape.230
  29.5 3.7 %all-to-all-start.1 = ((f32[4,1,3072]{2,1,0:T(1,128)}), f32[4,1,3072]{2,1,0:T(1,128)S(1)}, u32[]{:S(2)}, u32[]{:S(2)}) async-start(f32[4,1,3072]{2,1,0:T(1,128)} %reshape.230), calls=%async_computation.1 | async-start | bytes 98304 | tf_op jit(solution)/shard_map/all_to_all | solution.py:74
  33.4 4.0 %gather_fusion.1 = f32[512,384]{1,0:T(8,128)S(1)} fusion(f32[2,16,384]{2,1,0:T(8,128)S(1)} %reshape.189, s32[512]{0:T(512)S(1)} %bitcast.78), kind=kCustom, calls=%fused_computation.1 | custom fusion | bytes 1576960 | tf_op jit(solution)/shard_map/jit(take_along_axis)/gather | solution.py:72
  37.6 1.4 gather.21
  39.5 0.8 reduce.6
  40.5 8.5 %gather_fusion.2 = f32[2048,2,48]{2,1,0:T(2,128)S(1)} fusion(f32[8,16,2,48]{3,2,1,0:T(2,128)S(1)} %copy.86, s32[2048]{0:T(1024)S(1)} %bitcast.77), kind=kCustom, calls=%fused_computation.2 | custom fusion | bytes 1589248 | tf_op jit(solution)/shard_map/jit(take_along_axis)/gather | solution.py:75
  48.9 2.0 copy.88
  50.9 2.2 %fusion.36 = (f32[2,256]{1,0:T(2,128)S(1)}, f32[2,256,8,48]{1,0,3,2:T(2,128)S(1)}) fusion(f32[2,256,8,48]{1,0,3,2:T(2,128)} %gather.21, pred[2,256]{1,0:T(4,128)(4,1)S(1)} %compare_and_fusion.1, f32[8,256,2,48]{1,2,3,0:T(2,128)} %copy.88, pred[256,8]{0,1:T(8,128)(4,1)S(1)} %and_bitcast_fusion), kind=kLoop, calls=%fused_computation.74 | loop fusion | flops 785920 | bytes 2363904 | tf_op jit(solution)/shard_map/reduce_sum | solution.py:14
  54.9 3.7 %fusion.20 = (u8[256,1536]{1,0:T(8,128)(4,1)S(1)}, u8[256,1536]{1,0:T(8,128)(4,1)S(1)}, f32[2,256,1536]{2,1,0:T(8,128)S(1)}) fusion(bf16[384,2,1536]{2,0,1:T(8,128)(2,1)} %all-gather.3.cloned.1.call-done, f32[2,256,384]{2,1,0:T(8,128)S(1)} %subtract_multiply_fusion.1), kind=kOutput, calls=%fused_computation.54 | convolution fusion | flops 613613568 | bytes 7077888 | tf_op jit(solution)/shard_map/jbd,djf->jbf/dot_general | solution.py:83
  58.6 1.6 copy-done.4
  60.2 7.2 %fusion.2 = bf16[2,256,1536]{2,1,0:T(8,128)(2,1)S(1)} fusion(f32[2,256,1536]{2,1,0:T(8,128)S(1)} %get-tuple-element.30, u8[256,1536]{1,0:T(8,128)(4,1)S(1)} %get-tuple-element.21, u8[256,1536]{1,0:T(8,128)(4,1)S(1)} %get-tuple-element.20), kind=kLoop, calls=%fused_computation.9 | loop fusion | flops 55050240 | bytes 5505024 | tf_op jit(solution)/shard_map/convert_element_type | solution.py:84
  67.4 10.5 %all-gather.5.cloned.1.call-done = bf16[384,2,1536]{2,0,1:T(8,128)(2,1)} async-done(((bf16[48,2,1536]{2,0,1:T(8,128)(2,1)}), bf16[384,2,1536]{2,0,1:T(8,128)(2,1)}) %all-gather.5.cloned.1.call-update) | async-done | bytes 2359312 | tf_op jit(solution)/shard_map/all_gather | solution.py:81
  77.9 2.7 %fusion.52 = (f32[2,256]{1,0:T(2,128)S(1)}, f32[2,256,384]{2,1,0:T(8,128)S(1)}) fusion(f32[2,256,384]{2,1,0:T(8,128)S(1)} %copy-done.1, bf16[2,256,1536]{2,1,0:T(8,128)(2,1)S(1)} %fusion.2, bf16[384,2,1536]{2,0,1:T(8,128)(2,1)} %all-gather.5.cloned.1.call-done), kind=kOutput, calls=%fused_computation.114 | convolution fusion | flops 604372480 | bytes 5507072 | tf_op jit(solution)/shard_map/jbf,djf->jbd/dot_general | solution.py:85
  80.9 0.8 fusion.21
  81.8 9.6 %psum.7 = f32[256]{0:T(256)S(1)} all-reduce(f32[256]{0:T(256)S(1)} %bitcast.89), channel_id=1, replica_groups=mesh['tok'=4,'smp'=8] {'tok'}, use_global_device_ids=true, to_apply=%region_5.6 | all-reduce | flops 256 | bytes 2048 | tf_op jit(solution)/shard_map/psum | solution.py:88
  91.8 3.5 %convolution_bitcast_fusion = f32[384,2,1536]{0,2,1:T(8,128)} fusion(bf16[2,256,1536]{2,1,0:T(8,128)(2,1)S(1)} %fusion.2, f32[2,256,384]{2,1,0:T(8,128)S(1)} %get-tuple-element.32, f32[2,256]{1,0:T(2,128)S(1)} %get-tuple-element.36, f32[2,256]{1,0:T(2,128)S(1)} %get-tuple-element.37, f32[2,384]{1,0:T(2,128)S(1)} %copy-done.7, ...), kind=kOutput, calls=%fused_computation.5 | convolution fusion | flops 605552640 | bytes 7090176 | tf_op jit(solution)/shard_map/jbd,jbf->djf/dot_general | solution.py:94
  95.3 8.2 %copy.99 = f32[384,2,1536]{2,1,0:T(2,128)} copy(f32[384,2,1536]{0,2,1:T(8,128)} %convolution_bitcast_fusion) | data formatting | bytes 9437184 | tf_op jit(solution)/shard_map/jbd,jbf->djf/transpose | solution.py:94
  103.6 6.1 %fusion.51 = (f32[2,256]{1,0:T(2,128)S(1)}, f32[2,256]{1,0:T(2,128)S(1)}, f32[2,256,384]{2,1,0:T(8,128)S(1)}) fusion(f32[2,256,384]{2,1,0:T(8,128)S(1)} %copy-done.1, bf16[384,2,1536]{2,0,1:T(8,128)(2,1)} %all-gather.3.cloned.1.call-done, f32[2,256,1536]{2,1,0:T(8,128)} %copy-done.4, bf16[384,2,1536]{2,0,1:T(8,128)(2,1)} %all-gather.5.cloned.1.call-done, ...), kind=kOutput, calls=%fused_computation.113 | convolution fusion | flops 1219558400 | bytes 10240000 | tf_op jit(solution)/shard_map/jbf,djf->jbd/dot_general | solution.py:103
  110.9 0.8 reshape.232
  111.7 3.3 %all-to-all-start.2 = ((f32[4,1,3072]{2,1,0:T(1,128)}), f32[4,1,3072]{2,1,0:T(1,128)S(1)}, u32[]{:S(2)}, u32[]{:S(2)}) async-start(f32[4,1,3072]{2,1,0:T(1,128)} %reshape.232), calls=%async_computation.2 | async-start | bytes 98304 | tf_op jit(solution)/shard_map/all_to_all | solution.py:111
  115.1 4.7 %all-to-all-done.2 = f32[4,1,3072]{2,1,0:T(1,128)S(1)} async-done(((f32[4,1,3072]{2,1,0:T(1,128)}), f32[4,1,3072]{2,1,0:T(1,128)S(1)}, u32[]{:S(2)}, u32[]{:S(2)}) %all-to-all-start.2) | async-done | bytes 49184 | tf_op jit(solution)/shard_map/all_to_all | solution.py:111
  119.8 0.8 reduce.7
  122.0 3.3 %all-to-all-start.3 = ((f32[2,8,2,384]{3,2,0,1:T(2,128)}), f32[2,8,2,384]{3,2,0,1:T(2,128)S(1)}, u32[]{:S(2)}, u32[]{:S(2)}) async-start(f32[2,8,2,384]{3,2,0,1:T(2,128)} %copy.96), calls=%async_computation.3 | async-start | bytes 98304 | tf_op jit(solution)/shard_map/all_to_all | solution.py:116
  126.6 5.3 %all-to-all-done.3 = f32[2,8,2,384]{3,2,0,1:T(2,128)S(1)} async-done(((f32[2,8,2,384]{3,2,0,1:T(2,128)}), f32[2,8,2,384]{3,2,0,1:T(2,128)S(1)}, u32[]{:S(2)}, u32[]{:S(2)}) %all-to-all-start.3) | async-done | bytes 49184 | tf_op jit(solution)/shard_map/all_to_all | solution.py:116
  133.2 1.2 subtract_select_fusion.1
  134.4 74.3 %all-reduce.3.cloned.1.call-done = f32[384,2,1536]{2,1,0:T(2,128)} async-done(((f32[384,2,1536]{2,1,0:T(2,128)}), f32[384,2,1536]{2,1,0:T(2,128)}) %all-reduce.3.cloned.1.call-update) | async-done | bytes 4718608
  208.6 1.9 constant_dynamic-slice_fusion
  (96 shorter events, 13.4 us)
Async XLA Ops:
  7.2 15.7 %copy-start.8 = (s32[2,1,8]{2,1,0:T(1,128)S(1)}, s32[2,1,8]{2,1,0:T(1,128)}, u32[]{:S(2)}) copy-start(s32[2,1,8]{2,1,0:T(1,128)} %param.16) | copy-start | bytes 196
  7.2 14.8 %copy-start.5 = (bf16[48,2,1536]{2,1,0:T(2,128)(2,1)S(1)}, bf16[48,2,1536]{2,1,0:T(2,128)(2,1)}, u32[]{:S(2)}) copy-start(bf16[48,2,1536]{2,1,0:T(2,128)(2,1)} %param.20) | copy-start | bytes 884740
  7.2 15.6 %copy-start.6 = (s32[8,256]{1,0:T(8,128)S(1)}, s32[8,256]{1,0:T(8,128)}, u32[]{:S(2)}) copy-start(s32[8,256]{1,0:T(8,128)} %param.17) | copy-start | bytes 24580
  7.2 47.6 %all-gather.3.cloned.1.call-start = ((), (), s32[]{:S(2)}) async-start(), calls=%async_computation.4 | async-start | bytes 2654208 | tf_op jit(solution)/shard_map/all_gather | solution.py:80
  15.6 12.9 %all-to-all-start = ((f32[2,8,2,384]{3,2,0,1:T(2,128)}), f32[2,8,2,384]{3,2,0,1:T(2,128)S(1)}, u32[]{:S(2)}, u32[]{:S(2)}) async-start(f32[2,8,2,384]{3,2,0,1:T(2,128)} %fusion.31), calls=%async_computation | async-start | bytes 98304 | tf_op jit(solution)/shard_map/all_to_all | solution.py:62
  22.0 56.0 %all-gather.5.cloned.1.call-start = ((), (), s32[]{:S(2)}) async-start(), calls=%async_computation.5 | async-start | bytes 2654208 | tf_op jit(solution)/shard_map/all_gather | solution.py:81
  29.5 9.4 %all-to-all-start.1 = ((f32[4,1,3072]{2,1,0:T(1,128)}), f32[4,1,3072]{2,1,0:T(1,128)S(1)}, u32[]{:S(2)}, u32[]{:S(2)}) async-start(f32[4,1,3072]{2,1,0:T(1,128)} %reshape.230), calls=%async_computation.1 | async-start | bytes 98304 | tf_op jit(solution)/shard_map/all_to_all | solution.py:74
  33.2 175.4 %all-reduce.3.cloned.1.call-start = ((), (), s32[]{:S(2)}) async-start(), calls=%async_computation.6 | async-start | bytes 9437184
  50.9 2.9 %copy-start.2 = (f32[2,256,8,48]{1,0,3,2:T(2,128)S(1)}, f32[2,256,8,48]{1,0,3,2:T(2,128)}, u32[]{:S(2)}) copy-start(f32[2,256,8,48]{1,0,3,2:T(2,128)} %gather.21) | copy-start | bytes 2359300
  54.8 3.7 %copy-start = (f32[2,256,384]{2,1,0:T(8,128)}, f32[2,256,384]{2,1,0:T(8,128)S(1)}, u32[]{:S(2)}) copy-start(f32[2,256,384]{2,1,0:T(8,128)S(1)} %subtract_multiply_fusion.1) | copy-start | bytes 2359300
  58.5 1.6 copy-start.4
  58.5 19.4 %copy-start.1 = (f32[2,256,384]{2,1,0:T(8,128)S(1)}, f32[2,256,384]{2,1,0:T(8,128)}, u32[]{:S(2)}) copy-start(f32[2,256,384]{2,1,0:T(8,128)} %copy-done) | copy-start | bytes 2359300
  67.3 13.6 %copy-start.7 = (f32[2,384]{1,0:T(2,128)S(1)}, f32[2,384]{1,0:T(2,128)}, u32[]{:S(2)}) copy-start(f32[2,384]{1,0:T(2,128)} %param.21) | copy-start | bytes 9220
  67.4 24.0 %copy-start.11 = (s32[256]{0:T(256)S(1)}, s32[256]{0:T(256)}, u32[]{:S(2)}) copy-start(s32[256]{0:T(256)} %param.18) | copy-start | bytes 3076
  91.4 3.9 %copy-start.9 = (f32[256]{0:T(256)}, f32[256]{0:T(256)S(1)}, u32[]{:S(2)}) copy-start(f32[256]{0:T(256)S(1)} %psum.7) | copy-start | bytes 3076
  109.7 15.7 %copy-start.12 = (u32[32]{0:T(128)S(1)}, u32[32]{0:T(128)}, u32[]{:S(2)}) copy-start(u32[32]{0:T(128)} %constant.182) | copy-start | bytes 388
  110.0 22.7 %copy-start.10 = (f32[2,256]{1,0:T(2,128)S(1)}, f32[2,256]{1,0:T(2,128)}, u32[]{:S(2)}) copy-start(f32[2,256]{1,0:T(2,128)} %param.12) | copy-start | bytes 6148
  110.0 23.2 %copy-start.3 = (f32[2,256,384]{2,1,0:T(8,128)S(1)}, f32[2,256,384]{2,1,0:T(8,128)}, u32[]{:S(2)}) copy-start(f32[2,256,384]{2,1,0:T(8,128)} %param.11) | copy-start | bytes 2359300
  111.7 8.1 %all-to-all-start.2 = ((f32[4,1,3072]{2,1,0:T(1,128)}), f32[4,1,3072]{2,1,0:T(1,128)S(1)}, u32[]{:S(2)}, u32[]{:S(2)}) async-start(f32[4,1,3072]{2,1,0:T(1,128)} %reshape.232), calls=%async_computation.2 | async-start | bytes 98304 | tf_op jit(solution)/shard_map/all_to_all | solution.py:111
  122.0 9.9 %all-to-all-start.3 = ((f32[2,8,2,384]{3,2,0,1:T(2,128)}), f32[2,8,2,384]{3,2,0,1:T(2,128)S(1)}, u32[]{:S(2)}, u32[]{:S(2)}) async-start(f32[2,8,2,384]{3,2,0,1:T(2,128)} %copy.96), calls=%async_computation.3 | async-start | bytes 98304 | tf_op jit(solution)/shard_map/all_to_all | solution.py:116
Sparse Core Ops, SparseCore 0:
  10.2 35.5 all-gather.2
  47.4 30.4 all-gather.4
  103.7 104.9 all-reduce.2
where the time goes:
time: 218 us; the launch traced here: 217 us
  waiting for transfers between devices  100 us (46%)
  local copies, waits for them, and re-layouts  37.5 us (17%)
  other arithmetic  19 us (9%)
  matrix products  18.5 us (8%)
  starting transfers between devices  16.7 us (8%)
  between operations  15.5 us (7%)
  blocking collectives  9.62 us (4%)
    unnamed x4, waiting for transfers between devices  74.3 us
    all_gather x1, waiting for transfers between devices, on_device(): lax.all_gather(down_weight, 'smp', axis=0, tiled=True)  10.5 us
    gather x2, local copies, waits for them, and re-layouts, on_device(): jnp.take_along_axis(received, sample_slots[:, :, None, None], axis=1)  10.5 us
    psum x1, blocking collectives, on_device(): logits = lax.psum(partial_logit, 'tok')  9.62 us
    unnamed x37, local copies, waits for them, and re-layouts  9.21 us
    transpose x1, local copies, waits for them, and re-layouts, on_device(): jnp.einsum('jbd,jbf->djf', grad_out_bf, active, preferred_element_type=jn...  8.24 us
    convert_element_type x1, other arithmetic, on_device(): active = jax.nn.gelu(preact, approximate=False).astype(jnp.bfloat16)  7.18 us
    all_to_all x1, starting transfers between devices, on_device(): lax.all_to_all(looked.reshape(local_toks, group_count, capacity, model_wi...  6.33 us
  transfers between devices with their start and end apart: 7, of which 5 were waited for; matrix products, arithmetic and copies ran while one was open for 25% of the time, Pallas kernels for 0%

commit v1 on v0

v1 whole, which is shorter than its diff:
```python
import functools
import math

import jax
import jax.numpy as jnp
from jax import lax
from jax.experimental import pallas as pl
from jax.experimental.pallas import tpu as pltpu
from jax.sharding import PartitionSpec as P

decay_log = math.log(0.98)
learn_rate = 0.2
norm_eps = 1e-05
MESH = pl.DeviceIdType.MESH
VMEM = pltpu.VMEM


def normalize(values):
    centre = jnp.mean(values, axis=-1, keepdims=True)
    shifted = values - centre
    inverse = lax.rsqrt(jnp.mean(shifted * shifted, axis=-1, keepdims=True) + norm_eps)
    return (shifted * inverse, inverse)


def norm_back(grad_in, normed, inverse):
    first_mean = jnp.mean(grad_in, axis=-1, keepdims=True)
    second = jnp.mean(grad_in * normed, axis=-1, keepdims=True)
    return inverse * (grad_in - first_mean - normed * second)


def gelu_grad(preact):
    cumulative = 0.5 * (1.0 + lax.erf(preact * (1.0 / math.sqrt(2.0))))
    density = jnp.exp(-0.5 * preact * preact) * (1.0 / math.sqrt(2.0 * math.pi))
    return cumulative + preact * density


def greet(axes):
    barrier = pltpu.get_barrier_semaphore()
    total = 0
    for name, size in axes:
        me = lax.axis_index(name)
        for k in range(1, size):
            pl.semaphore_signal(barrier, inc=1, device_id={name: lax.rem(me + k, size)}, device_id_type=MESH)
        total += size - 1
    pl.semaphore_wait(barrier, total)


def send_all(name, size, source, target, send_sem, recv_sem):
    me = lax.axis_index(name)
    copies = []
    for k in range(1, size):
        peer = lax.rem(me + k, size)
        copy = pltpu.make_async_remote_copy(
            src_ref=source(peer),
            dst_ref=target,
            send_sem=send_sem.at[k],
            recv_sem=recv_sem.at[k],
            device_id={name: peer},
            device_id_type=MESH,
        )
        copy.start()
        copies.append(copy)
    return copies


def lists_kernel(n_tok, n_smp, x_ref, y_ref, send_a, recv_a, send_b, recv_b):
    tok, smp = lax.axis_index("tok"), lax.axis_index("smp")
    greet((("smp", n_smp), ("tok", n_tok)))
    copies = send_all("smp", n_smp, lambda p: x_ref.at[p], y_ref.at[tok, smp], send_a, recv_a)
    y_ref[tok, smp] = x_ref[smp]
    for copy in copies:
        copy.wait()
    for copy in send_all("tok", n_tok, lambda p: y_ref.at[tok], y_ref.at[tok], send_b, recv_b):
        copy.wait()


def grads_kernel(n_tok, n_smp, s_ref, y_ref, landed, total, send_a, recv_a, send_b, recv_b):
    tok, smp = lax.axis_index("tok"), lax.axis_index("smp")
    greet((("smp", n_smp), ("tok", n_tok)))
    copies = send_all("tok", n_tok, lambda p: s_ref.at[p], landed.at[tok], send_a, recv_a)
    landed[tok] = s_ref[tok]
    for copy in copies:
        copy.wait()
    total[...] = jnp.sum(landed[...], axis=0)
    copies = send_all("smp", n_smp, lambda p: total.at[p], y_ref.at[smp], send_b, recv_b)
    y_ref[smp] = total[smp]
    for copy in copies:
        copy.wait()


def logits_kernel(n_tok, x_ref, y_ref, landed, send_sem, recv_sem):
    tok = lax.axis_index("tok")
    greet((("tok", n_tok),))
    copies = send_all("tok", n_tok, lambda p: x_ref, landed.at[tok], send_sem, recv_sem)
    landed[tok] = x_ref[...]
    for copy in copies:
        copy.wait()
    y_ref[...] = jnp.sum(landed[...], axis=0)


def call(kernel, operand, out_shape, scratch, sems, ident):
    return pl.pallas_call(
        kernel,
        out_shape=jax.ShapeDtypeStruct(out_shape, jnp.float32),
        in_specs=[pl.BlockSpec(memory_space=VMEM)],
        out_specs=pl.BlockSpec(memory_space=VMEM),
        scratch_shapes=[VMEM(s, jnp.float32) for s in scratch]
        + [pltpu.SemaphoreType.DMA((n,)) for n in sems],
        compiler_params=pltpu.CompilerParams(
            collective_id=ident, has_side_effects=True, vmem_limit_bytes=24 << 20
        ),
        cost_estimate=pl.CostEstimate(flops=0, bytes_accessed=30_000_000, transcendentals=0),
    )(operand)


def on_device(
    n_tok,
    n_smp,
    row_table,
    row_accum,
    last_step,
    step_now,
    row_ids,
    row_counts,
    sample_slots,
    labels,
    up_weight,
    down_weight,
    out_weight,
):
    highest = lax.Precision.HIGHEST
    local_toks, shard_rows, width = row_table.shape
    groups, capacity = row_ids.shape[2:]
    batch = labels.shape[0]
    toks = sample_slots.shape[0]
    head = width // toks
    rows = local_toks * capacity
    flat = n_tok * n_smp * rows
    tok, smp = lax.axis_index("tok"), lax.axis_index("smp")

    up_full = lax.all_gather(up_weight, "smp", axis=0, tiled=True)
    down_full = lax.all_gather(down_weight, "smp", axis=0, tiled=True)

    factor = jnp.exp((step_now[0] - last_step).astype(jnp.float32) * decay_log)
    ids = row_ids[:, 0].transpose(1, 0, 2)
    valid = jnp.arange(capacity)[None, None, :] < row_counts[:, 0].T[:, :, None]
    pick = ids[..., None] == jnp.arange(shard_rows)
    looked = jnp.einsum(
        "gjcr,jrd->gjcd", pick.astype(jnp.float32), row_table * factor[:, :, None], precision=highest
    ).reshape(groups, rows, width)
    lists = call(
        functools.partial(lists_kernel, n_tok, n_smp),
        looked,
        (n_tok, n_smp, rows, width),
        [],
        [n_smp, n_smp, n_tok, n_tok],
        1,
    ).reshape(flat, width)

    place = jnp.arange(n_smp)[:, None] * capacity + jnp.arange(capacity)
    slots = sample_slots.reshape(n_tok, 1, local_toks, 1, batch)
    hits = (slots == place[None, :, None, :, None]).astype(jnp.float32).reshape(flat, batch)
    number = jnp.arange(flat)
    token = number // (n_smp * rows) * local_toks + number % rows // capacity
    block = token[:, None] == (jnp.arange(width) // head)[None, :]
    mine = [(token == tok * local_toks + j)[:, None] for j in range(local_toks)]

    gathered = []
    for j in range(local_toks):
        part = lax.dynamic_slice_in_dim(lists, (tok * local_toks + j) * head, head, 1)
        spread = jnp.where(block, jnp.tile(part, (1, toks)), 0.0)
        gathered.append(spread + jnp.where(mine[j], lists, 0.0))
    summed = jnp.einsum("kb,jkd->jbd", hits, jnp.stack(gathered), precision=highest)
    normed_in, inverse_in = normalize(summed)
    input_bf = normed_in.astype(jnp.bfloat16)
    preact = jnp.einsum("jbd,djf->jbf", input_bf, up_full, preferred_element_type=jnp.float32)
    active = jax.nn.gelu(preact, approximate=False).astype(jnp.bfloat16)
    output = jnp.einsum("jbf,djf->jbd", active, down_full, preferred_element_type=jnp.float32)
    normed_out, inverse_out = normalize(normed_in + output)
    partial_logit = jnp.sum(normed_out * out_weight[:, None, :], axis=(0, 2))
    logits = call(
        functools.partial(logits_kernel, n_tok),
        partial_logit.reshape(1, batch),
        (1, batch),
        [(n_tok, 1, batch)],
        [n_tok, n_tok],
        2,
    ).reshape(batch)
    dlogit = jax.nn.sigmoid(logits) - labels.astype(jnp.float32)
    grad_sum = norm_back(dlogit[None, :, None] * out_weight[:, None, :], normed_out, inverse_out)
    grad_out_bf = grad_sum.astype(jnp.bfloat16)

    near = 2 if n_smp % 2 == 0 else 1
    far = n_smp // near
    partial = jnp.einsum("jbd,jbf->jdf", grad_out_bf, active, preferred_element_type=jnp.float32)
    partial = partial.reshape(local_toks, far, near, width // n_smp, -1)
    z, core = smp // near, smp % near
    pair = lax.dynamic_index_in_dim(partial, core, 2, keepdims=False)
    if near == 2:
        other = lax.dynamic_index_in_dim(partial, 1 - core, 2, keepdims=False)
        pair = pair + lax.ppermute(other, "smp", [(i, i ^ 1) for i in range(n_smp)])
    def far_sums(pair):
        grad_down = lax.dynamic_index_in_dim(pair, z, 1, keepdims=False)
        flip = far & (far - 1) == 0
        for k in range(far - 1, 0, -1):
            partner = z ^ k if flip else (z + k) % far
            part = lax.dynamic_index_in_dim(pair, partner, 1, keepdims=False)
            if not (flip and k == 1):
                part = part.astype(jnp.bfloat16)
            route = [(i, i ^ (k * near) if flip else (i + k * near) % n_smp) for i in range(n_smp)]
            grad_down = grad_down + lax.ppermute(part, "smp", route).astype(jnp.float32)
        return grad_down.transpose(1, 0, 2)

    grad_active = jnp.einsum(
        "jbd,djf->jbf", grad_out_bf, down_full, preferred_element_type=jnp.float32
    )
    grad_pre = (grad_active * gelu_grad(preact)).astype(jnp.bfloat16)
    grad_normed = grad_sum + jnp.einsum(
        "jbf,djf->jbd", grad_pre, up_full, preferred_element_type=jnp.float32
    )
    grad_mixed = norm_back(grad_normed, normed_in, inverse_in)
    pair, grad_mixed = lax.optimization_barrier((pair, grad_mixed))
    grad_down = far_sums(pair)

    sums = jnp.einsum("kb,jbd->jkd", hits, grad_mixed, precision=highest)
    sent = jnp.zeros((flat, width), jnp.float32)
    for j in range(local_toks):
        own_head = (jnp.arange(width) // head == tok * local_toks + j)[None, :]
        heads = jnp.where(block, sums[j], 0.0).reshape(flat, toks, head).sum(axis=1)
        sent = sent + jnp.where(own_head, jnp.tile(heads, (1, toks)), 0.0)
        sent = sent + jnp.where(mine[j], sums[j], 0.0)
    back = call(
        functools.partial(grads_kernel, n_tok, n_smp),
        sent.reshape(n_tok, n_smp, rows, width),
        (n_smp, rows, width),
        [(n_tok, n_smp, rows, width), (n_smp, rows, width)],
        [n_tok, n_tok, n_smp, n_smp],
        3,
    ).reshape(groups, local_toks, capacity, width)

    taken = (pick & valid[..., None]).astype(jnp.float32)
    row_grads = jnp.einsum("gjcr,gjcd->jrd", taken, back, precision=highest)
    touched = jnp.sum(taken, axis=(0, 2)) > 0.0
    new_accum = row_accum + jnp.mean(row_grads * row_grads, axis=2)
    updated = row_table * factor[:, :, None] - learn_rate * row_grads * lax.rsqrt(new_accum)[:, :, None]
    new_table = jnp.where(touched[:, :, None], updated, row_table)
    return (new_table, new_accum, grad_down, logits)


def solution(mesh):
    return jax.shard_map(
        functools.partial(on_device, mesh.shape["tok"], mesh.shape["smp"]),
        mesh=mesh,
        in_specs=(
            P("tok", "smp", None),
            P("tok", "smp"),
            P("tok", "smp"),
            P(),
            P("tok", "smp", None, None),
            P("tok", "smp", None),
            P(None, "smp"),
            P("smp"),
            P("smp", "tok", None),
            P("smp", "tok", None),
            P("tok", None),
        ),
        out_specs=(P("tok", "smp", None), P("tok", "smp"), P("smp", "tok", None), P("smp")),
        check_vma=False,
    )
```

time: 218 us -> 148 us (0.68)
  waiting for transfers between devices: 100 us -> 36.3 us
  Pallas kernels: 0 us -> 43.4 us
  local copies, waits for them, and re-layouts: 37.5 us -> 15.8 us
  starting transfers between devices: 16.7 us -> 3.64 us
  blocking collectives: 9.62 us -> 0 us
  matrix products: 18.5 us -> 15.4 us
    unnamed x4 -> x2, waiting for transfers between devices: 74.3 us -> 0.03 us
    pallas_call x0 -> x3, Pallas kernels: none -> 43.4 us  [call(): pl.pallas_call(kernel, out_shape=jax.ShapeDtypeStruct(out_shape, jnp.floa...]
    all_gather x2, waiting for transfers between devices: 10.6 us -> 36.3 us  [the longest x1 20.5 us: on_device(): down_full = lax.all_gather(down_weight, 'smp', axis=0, tiled=True)]
    gather x8 -> x0, local copies, waits for them, and re-layouts: 16.9 us -> none  [the longest x2 10.5 us: on_device(): jnp.take_along_axis(received, sample_slots[:, :, None, None], axis=1)]
    all_to_all x4 -> x0, starting transfers between devices: 16.6 us -> none  [the longest x1 6.33 us: on_device(): lax.all_to_all(looked.reshape(local_toks, group_count, capacity, model_wi...]
    all_to_all x4 -> x0, waiting for transfers between devices: 15.4 us -> none  [the longest x1 5.43 us: on_device(): lax.all_to_all(looked.reshape(local_toks, group_count, capacity, model_wi...]
    psum x1 -> x0, blocking collectives: 9.62 us -> none  [on_device(): logits = lax.psum(partial_logit, 'tok')]
    transpose x1 -> x0, local copies, waits for them, and re-layouts: 8.24 us -> none  [on_device(): jnp.einsum('jbd,jbf->djf', grad_out_bf, active, preferred_element_type=jn...]
  transfers between devices with their start and end apart: 7 -> 6, of which waited for: 5 -> 2; matrix products, arithmetic and copies ran while one was open for 25% -> 19% of each run, Pallas kernels for 0% -> 26%
where the time goes in v1:
time: 148 us
  Pallas kernels  43.4 us (29%)
  waiting for transfers between devices  36.3 us (25%)
  other arithmetic  18 us (12%)
  local copies, waits for them, and re-layouts  15.8 us (11%)
  matrix products  15.4 us (10%)
  between operations  15.2 us (10%)
  starting transfers between devices  3.64 us (2%)
    pallas_call x3, Pallas kernels, call(): pl.pallas_call(kernel, out_shape=jax.ShapeDtypeStruct(out_shape, jnp.floa...  43.4 us
    all_gather x1, waiting for transfers between devices, on_device(): down_full = lax.all_gather(down_weight, 'smp', axis=0, tiled=True)  20.5 us
    all_gather x1, waiting for transfers between devices, on_device(): up_full = lax.all_gather(up_weight, 'smp', axis=0, tiled=True)  15.8 us
    unnamed x23, local copies, waits for them, and re-layouts  7.4 us
    convert_element_type x1, other arithmetic, on_device(): active = jax.nn.gelu(preact, approximate=False).astype(jnp.bfloat16)  7.18 us
    dot_general x1, matrix products, on_device(): jnp.einsum('jbf,djf->jbd', grad_pre, up_full, preferred_element_type=jnp....  5.24 us
    add x1, other arithmetic, on_device(): pair = pair + lax.ppermute(other, 'smp', [(i, i ^ 1) for i in range(n_smp)])  4.13 us
    dot_general x1, matrix products, on_device(): jnp.einsum('jbd,djf->jbf', input_bf, up_full, preferred_element_type=jnp....  3.59 us
  transfers between devices with their start and end apart: 6, of which 2 were waited for; matrix products, arithmetic and copies ran while one was open for 19% of the time, Pallas kernels for 26%

profile of v1, /device:TPU:0, one launch (start us, length us, event | category | flops | bytes accessed | tf_op | source)
XLA Modules:
  0.0 147.8 jit_solution(16990740916077343290)
XLA Ops:
  7.2 1.7 %copy.50 = bf16[48,2,1536]{2,0,1:T(8,128)(2,1)} copy(bf16[48,2,1536]{2,1,0:T(2,128)(2,1)} %param.19) | data formatting | bytes 589824 | tf_op args[8]
  9.0 1.7 %copy.52 = bf16[48,2,1536]{2,0,1:T(8,128)(2,1)} copy(bf16[48,2,1536]{2,1,0:T(2,128)(2,1)} %param.20) | data formatting | bytes 589824 | tf_op args[9]
  11.4 0.7 multiply_exponential_fusion
  12.1 1.6 %fusion.17 = f32[2,384,8,2]{1,2,3,0:T(8,128)S(1)} fusion(f32[2,256,384]{2,1,0:T(8,128)} %param.11, f32[2,256]{1,0:T(2,128)S(1)} %multiply_exponential_fusion, s32[8,2,2]{0,2,1:T(2,128)} %bitcast.77), kind=kOutput, calls=%fused_computation.42 | convolution fusion | flops 37953536 | bytes 837760 | tf_op jit(solution)/shard_map/gjcr,jrd->gjcd/dot_general | solution.py:148
  13.7 13.1 %shard_map.138 = f32[4,8,4,384]{3,2,1,0:T(4,128)S(1)} custom-call(f32[8,4,384]{2,1,0:T(4,128)S(1)} %copy.69.x_ref), custom_call_target="tpu_custom_call" | custom-call | bytes 30000000 | tf_op jit(solution)/shard_map/pallas_call | solution.py:102
  28.1 0.5 fusion.75
  28.7 15.8 %all-gather.3.cloned.1.call-done = bf16[384,2,1536]{2,0,1:T(8,128)(2,1)} async-done(((bf16[48,2,1536]{2,0,1:T(8,128)(2,1)}), bf16[384,2,1536]{2,0,1:T(8,128)(2,1)}) %all-gather.3.cloned.1.call-update) | async-done | bytes 2359312 | tf_op jit(solution)/shard_map/all_gather | solution.py:141
  44.5 3.6 %fusion.20 = (u8[256,1536]{1,0:T(8,128)(4,1)S(1)}, u8[256,1536]{1,0:T(8,128)(4,1)S(1)}, f32[2,256,1536]{2,1,0:T(8,128)S(1)}) fusion(bf16[384,2,1536]{2,0,1:T(8,128)(2,1)} %all-gather.3.cloned.1.call-done, f32[2,256,384]{1,2,0:T(8,128)S(1)} %get-tuple-element.29, f32[2,256]{1,0:T(2,128)S(1)} %add_rsqrt_fusion.1, f32[2,256]{1,0:T(2,128)S(1)} %broadcast_multiply_fusion.5), kind=kOutput, calls=%fused_computation.52 | convolution fusion | flops 614006784 | bytes 7081984 | tf_op jit(solution)/shard_map/jbd,djf->jbf/dot_general | solution.py:176
  48.1 1.7 %copy-done.3 = f32[2,256,1536]{2,1,0:T(8,128)} copy-done((f32[2,256,1536]{2,1,0:T(8,128)}, f32[2,256,1536]{2,1,0:T(8,128)S(1)}, u32[]{:S(2)}) %copy-start.3) | copy-done | bytes 3145752
  49.8 7.2 %fusion.2 = bf16[2,256,1536]{2,1,0:T(8,128)(2,1)S(1)} fusion(f32[2,256,1536]{2,1,0:T(8,128)S(1)} %get-tuple-element.30, u8[256,1536]{1,0:T(8,128)(4,1)S(1)} %get-tuple-element.9, u8[256,1536]{1,0:T(8,128)(4,1)S(1)} %get-tuple-element.8), kind=kLoop, calls=%fused_computation.5 | loop fusion | flops 55050240 | bytes 5505024 | tf_op jit(solution)/shard_map/convert_element_type | solution.py:177
  57.0 20.5 %all-gather.5.cloned.1.call-done = bf16[384,2,1536]{2,0,1:T(8,128)(2,1)} async-done(((bf16[48,2,1536]{2,0,1:T(8,128)(2,1)}), bf16[384,2,1536]{2,0,1:T(8,128)(2,1)}) %all-gather.5.cloned.1.call-update) | async-done | bytes 2359312 | tf_op jit(solution)/shard_map/all_gather | solution.py:142
  77.5 2.5 %fusion.76 = (f32[2,256]{1,0:T(2,128)S(1)}, f32[2,256,384]{1,2,0:T(8,128)S(1)}) fusion(bf16[2,256,1536]{2,1,0:T(8,128)(2,1)S(1)} %fusion.2, bf16[384,2,1536]{2,0,1:T(8,128)(2,1)} %all-gather.5.cloned.1.call-done, f32[2,256]{1,0:T(2,128)S(1)} %add_rsqrt_fusion.1, f32[2,256,384]{1,2,0:T(8,128)S(1)} %get-tuple-element.29, ...), kind=kOutput, calls=%fused_computation.171 | convolution fusion | flops 604765696 | bytes 5511168 | tf_op jit(solution)/shard_map/jbf,djf->jbd/dot_general | solution.py:178
  80.3 4.6 %shard_map.139 = f32[1,256]{1,0:T(1,128)S(1)} custom-call(f32[1,256]{1,0:T(1,128)S(1)} %bitcast.71), custom_call_target="tpu_custom_call" | custom-call | bytes 30000000 | tf_op jit(solution)/shard_map/pallas_call | solution.py:102
  85.2 0.8 fusion.39
  86.0 1.9 %constant_dynamic-slice_fusion.1 = (f32[2,4,1,48,1536]{4,3,2,1,0:T(8,128)}, f32[2,4,1,48,1536]{4,3,2,1,0:T(8,128)S(1)}) fusion(f32[2,4,2,48,1536]{4,3,2,1,0:T(8,128)S(1)} %bitcast.72, s32[]{:T(128)S(6)} %select_n.248, s32[]{:T(128)S(6)} %select_n.249), kind=kLoop, calls=%fused_computation.131 | loop fusion | bytes 9437192 | tf_op jit(solution)/shard_map/jit(dynamic_index_in_dim)/dynamic_slice | solution.py:198
  87.9 3.3 %copy.73 = f32[2,4,1,48,1536]{4,0,3,1,2:T(2,128)} copy(f32[2,4,1,48,1536]{4,3,2,1,0:T(8,128)S(1)} %get-tuple-element.19) | data formatting | bytes 4718592 | tf_op jit(solution)/shard_map/jit(dynamic_index_in_dim)/dynamic_slice | solution.py:200
  91.5 5.2 %fusion.73 = (f32[2,256]{1,0:T(2,128)S(1)}, f32[2,256]{1,0:T(2,128)S(1)}, f32[2,256,384]{1,2,0:T(8,128)S(1)}) fusion(f32[2,256]{1,0:T(2,128)S(1)} %add_rsqrt_fusion.1, f32[2,256,384]{1,2,0:T(8,128)S(1)} %get-tuple-element.29, f32[2,256]{1,0:T(2,128)S(1)} %broadcast_multiply_fusion.5, bf16[384,2,1536]{2,0,1:T(8,128)(2,1)} %all-gather.3.cloned.1.call-done, ...), kind=kOutput, calls=%fused_computation.168 | convolution fusion | flops 1219951616 | bytes 10244096 | tf_op jit(solution)/shard_map/jbf,djf->jbd/dot_general | solution.py:218
  96.9 1.5 copy-done
  98.4 4.1 %bitcast_add_fusion = f32[2,4,48,1536]{3,0,2,1:T(2,128)S(1)} fusion(f32[2,4,48,1536]{3,0,2,1:T(2,128)} %collective-permute-done, f32[2,4,1,48,1536]{4,3,2,1,0:T(8,128)S(1)} %copy-done), kind=kLoop, calls=%fused_computation.29 | loop fusion | flops 589824 | bytes 7077888 | tf_op jit(solution)/shard_map/add | solution.py:201
  102.6 1.1 collective-permute-start.3
  103.6 0.3 copy-done.1
  103.9 1.2 fusion.35
  105.1 1.7 %collective-permute-start.1 = (bf16[2,48,1536]{2,0,1:T(2,128)(2,1)}, bf16[2,48,1536]{2,0,1:T(2,128)(2,1)}, u32[]{:S(2)}, u32[]{:S(2)}) collective-permute-start(bf16[2,48,1536]{2,0,1:T(2,128)(2,1)} %get-tuple-element.20), channel_id=1, source_target_pairs={{0,6},{1,7},{2,4},{3,5},{4,2},{5,3},{6,0},{7,1},{8,14},{9,15},{10,... | collective-permute-start | bytes 884744 | tf_op jit(solution)/shard_map/ppermute | solution.py:211
  106.9 0.8 collective-permute-start.2
  107.6 0.5 convolution_bitcast_fusion.2
  108.7 0.2 tile.41
  109.7 25.7 %shard_map.140 = f32[8,4,384]{2,1,0:T(4,128)S(1)} custom-call(f32[4,8,4,384]{3,2,1,0:T(4,128)S(1)} %select_add_fusion.s_ref), custom_call_target="tpu_custom_call" | custom-call | bytes 30000000 | tf_op jit(solution)/shard_map/pallas_call | solution.py:102
  135.4 0.7 multiply_reduce_fusion.1
  136.0 0.6 rsqrt_multiply_fusion
  136.6 1.2 subtract_select_fusion.1
  137.8 2.6 %fusion.24 = f32[48,2,1536]{2,1,0:T(2,128)} fusion(f32[2,48,1536]{2,0,1:T(2,128)S(1)} %collective-permute-done.3, bf16[2,48,1536]{2,0,1:T(2,128)(2,1)} %collective-permute-done.2, bf16[2,48,1536]{2,0,1:T(2,128)(2,1)} %collective-permute-done.1, f32[2,4,48,1536]{3,0,2,1:T(2,128)} %copy-done.1, s32[]{:T(128)S(6)} %select_n.261), kind=kLoop, calls=%fused_computation.59 | loop fusion | flops 737280 | bytes 2359300 | tf_op jit(solution)/shard_map/transpose | solution.py:212
  140.4 0.6 copy.79
  (81 shorter events, 3.6 us)
Async XLA Ops:
  7.2 20.3 %copy-start.6 = (s32[8,256]{1,0:T(8,128)S(1)}, s32[8,256]{1,0:T(8,128)}, u32[]{:S(2)}) copy-start(s32[8,256]{1,0:T(8,128)} %param.17) | copy-start | bytes 24580
  7.2 37.4 %all-gather.3.cloned.1.call-start = ((), (), s32[]{:S(2)}) async-start(), calls=%async_computation | async-start | bytes 2654208 | tf_op jit(solution)/shard_map/all_gather | solution.py:141
  9.0 68.5 %all-gather.5.cloned.1.call-start = ((), (), s32[]{:S(2)}) async-start(), calls=%async_computation.1 | async-start | bytes 2654208 | tf_op jit(solution)/shard_map/all_gather | solution.py:142
  48.1 1.7 %copy-start.3 = (f32[2,256,1536]{2,1,0:T(8,128)}, f32[2,256,1536]{2,1,0:T(8,128)S(1)}, u32[]{:S(2)}) copy-start(f32[2,256,1536]{2,1,0:T(8,128)S(1)} %get-tuple-element.30) | copy-start | bytes 9437188
  57.0 23.1 %copy-start.4 = (f32[2,384]{1,0:T(2,128)S(1)}, f32[2,384]{1,0:T(2,128)}, u32[]{:S(2)}) copy-start(f32[2,384]{1,0:T(2,128)} %param.21) | copy-start | bytes 9220
  57.0 27.9 %copy-start.8 = (s32[256]{0:T(256)S(1)}, s32[256]{0:T(256)}, u32[]{:S(2)}) copy-start(s32[256]{0:T(256)} %param.18) | copy-start | bytes 3076
  87.9 3.4 %copy-start.9 = (s32[2,1,8]{2,1,0:T(1,128)S(1)}, s32[2,1,8]{2,1,0:T(1,128)}, u32[]{:S(2)}) copy-start(s32[2,1,8]{2,1,0:T(1,128)} %param.16) | copy-start | bytes 196
  87.9 3.4 %copy-start.5 = (s32[2,1,8,2]{2,3,1,0:T(2,128)S(1)}, s32[2,1,8,2]{2,3,1,0:T(2,128)}, u32[]{:S(2)}) copy-start(s32[2,1,8,2]{2,3,1,0:T(2,128)} %param.15) | copy-start | bytes 388
  91.2 5.7 %collective-permute-start = (f32[2,4,48,1536]{3,0,2,1:T(2,128)}, f32[2,4,48,1536]{3,0,2,1:T(2,128)}, u32[]{:S(2)}, u32[]{:S(2)}) collective-permute-start(f32[2,4,48,1536]{3,0,2,1:T(2,128)} %bitcast.67), channel_id=1, source_target_pairs={{0,1},{1,0},{2,3},{3,2},{4,5},{5,4},{6,7},{7,6},{8,9},{9,8},{10,11... | collective-permute-start | bytes 7077896 | tf_op jit(solution)/shard_map/ppermute | solution.py:201
  96.7 1.7 %copy-start = (f32[2,4,1,48,1536]{4,3,2,1,0:T(8,128)S(1)}, f32[2,4,1,48,1536]{4,3,2,1,0:T(8,128)}, u32[]{:S(2)}) copy-start(f32[2,4,1,48,1536]{4,3,2,1,0:T(8,128)} %get-tuple-element.18) | copy-start | bytes 7077892
  102.5 1.4 copy-start.1
  102.6 35.2 %collective-permute-start.3 = (f32[2,48,1536]{2,0,1:T(2,128)S(1)}, f32[2,48,1536]{2,0,1:T(2,128)S(1)}, u32[]{:S(2)}, u32[]{:S(2)}) collective-permute-start(f32[2,48,1536]{2,0,1:T(2,128)S(1)} %dynamic-slice_bitcast_fusion), channel_id=1, source_target_pairs={{0,2},{1,3},{2,0},{3,1},{4,6},{5,7},{6,4},{7,5},{8,10},{9,11},{10,... | collective-permute-start | bytes 1769480 | tf_op jit(solution)/shard_map/ppermute | solution.py:211
  105.1 32.7 %collective-permute-start.1 = (bf16[2,48,1536]{2,0,1:T(2,128)(2,1)}, bf16[2,48,1536]{2,0,1:T(2,128)(2,1)}, u32[]{:S(2)}, u32[]{:S(2)}) collective-permute-start(bf16[2,48,1536]{2,0,1:T(2,128)(2,1)} %get-tuple-element.20), channel_id=1, source_target_pairs={{0,6},{1,7},{2,4},{3,5},{4,2},{5,3},{6,0},{7,1},{8,14},{9,15},{10,... | collective-permute-start | bytes 884744 | tf_op jit(solution)/shard_map/ppermute | solution.py:211
  106.9 30.9 %collective-permute-start.2 = (bf16[2,48,1536]{2,0,1:T(2,128)(2,1)}, bf16[2,48,1536]{2,0,1:T(2,128)(2,1)}, u32[]{:S(2)}, u32[]{:S(2)}) collective-permute-start(bf16[2,48,1536]{2,0,1:T(2,128)(2,1)} %get-tuple-element.21), channel_id=1, source_target_pairs={{0,4},{1,5},{2,6},{3,7},{4,0},{5,1},{6,2},{7,3},{8,12},{9,13},{10,... | collective-permute-start | bytes 884744 | tf_op jit(solution)/shard_map/ppermute | solution.py:211
  108.4 27.6 %copy-start.7 = (f32[2,256]{1,0:T(2,128)S(1)}, f32[2,256]{1,0:T(2,128)}, u32[]{:S(2)}) copy-start(f32[2,256]{1,0:T(2,128)} %param.12) | copy-start | bytes 6148
  108.4 28.2 %copy-start.2 = (f32[2,256,384]{2,1,0:T(8,128)S(1)}, f32[2,256,384]{2,1,0:T(8,128)}, u32[]{:S(2)}) copy-start(f32[2,256,384]{2,1,0:T(8,128)} %param.11) | copy-start | bytes 2359300
Sparse Core Ops, SparseCore 0:
  10.2 34.3 all-gather.2
  46.7 30.7 all-gather.4

commit v2 on v1

--- a/solution.py
+++ b/solution.py
@@ -63,14 +63,99 @@
     return copies
 
 
-def lists_kernel(n_tok, n_smp, x_ref, y_ref, send_a, recv_a, send_b, recv_b):
+def lists_kernel(
+    n_tok, n_smp, near, x_ref, w_ref, y_ref, up_ref, send_a, recv_a, send_b, recv_b, hop_send, hop_recv, swap_send, swap_recv
+):
     tok, smp = lax.axis_index("tok"), lax.axis_index("smp")
+    z, core = smp // near, lax.rem(smp, near)
+    far = n_smp // near
+    local_toks = w_ref.shape[0]
+    chunks = [(j, way) for j in range(local_toks) for way in (0, 1)]
+
+    def hop(j, way, step):
+        sign = 1 - 2 * way
+        block = up_ref.at[j, (z - sign * (step - 1) + far) % far * near + core]
+        return pltpu.make_async_remote_copy(
+            src_ref=block,
+            dst_ref=block,
+            send_sem=hop_send.at[j, way, step],
+            recv_sem=hop_recv.at[j, way, step],
+            device_id={"smp": (z + sign + far) % far * near + core},
+            device_id_type=MESH,
+        )
+
+    def leaves(way, step):
+        return (z >= step - 1) & (z + 1 < far) if way == 0 else (z + step - 1 < far) & (z >= 1)
+
+    def lands(way, step):
+        return z >= step if way == 0 else z + step < far
+
+    def swap(j, position):
+        block = up_ref.at[j, position * near + core]
+        return pltpu.make_async_remote_copy(
+            src_ref=block,
+            dst_ref=block,
+            send_sem=swap_send.at[j, position],
+            recv_sem=swap_recv.at[j, position],
+            device_id={"smp": z * near + near - 1 - core},
+            device_id_type=MESH,
+        )
+
+    def arrived(j, way, step):
+        sign = 1 - 2 * way
+        block = up_ref.at[j, (z - sign * step + far) % far * near + core]
+        pltpu.make_async_remote_copy(
+            src_ref=block,
+            dst_ref=block,
+            send_sem=hop_send.at[j, way, step],
+            recv_sem=hop_recv.at[j, way, step],
+            device_id={"smp": (z + sign + far) % far * near + core},
+            device_id_type=MESH,
+        ).wait_recv()
+
+    for j in range(local_toks):
+        up_ref[j, smp] = w_ref[j]
     greet((("smp", n_smp), ("tok", n_tok)))
     copies = send_all("smp", n_smp, lambda p: x_ref.at[p], y_ref.at[tok, smp], send_a, recv_a)
+    for j, way in chunks:
+        pl.when(leaves(way, 1))(lambda j=j, way=way: hop(j, way, 1).start())
+    if near == 2:
+        for j in range(local_toks):
+            swap(j, z).start()
     y_ref[tok, smp] = x_ref[smp]
     for copy in copies:
         copy.wait()
-    for copy in send_all("tok", n_tok, lambda p: y_ref.at[tok], y_ref.at[tok], send_b, recv_b):
+    copies = send_all("tok", n_tok, lambda p: y_ref.at[tok], y_ref.at[tok], send_b, recv_b)
+
+    def relay(step, carry):
+        for j, way in chunks:
+
+            @pl.when(lands(way, step))
+            def _(j=j, way=way):
+                arrived(j, way, step)
+                pl.when((step + 1 < far) & leaves(way, step + 1))(lambda: hop(j, way, step + 1).start())
+                if near == 2:
+                    swap(j, z - step if way == 0 else z + step).start()
+
+        return carry
+
+    lax.fori_loop(1, far, relay, 0)
+
+    def finish(step, carry):
+        for j, way in chunks:
+            pl.when(leaves(way, step))(lambda j=j, way=way: hop(j, way, step).wait_send())
+        return carry
+
+    lax.fori_loop(1, far, finish, 0)
+    if near == 2:
+
+        def swapped(position, carry):
+            for j in range(local_toks):
+                swap(j, position).wait()
+            return carry
+
+        lax.fori_loop(0, far, swapped, 0)
+    for copy in copies:
         copy.wait()
 
 
@@ -138,7 +223,6 @@
     flat = n_tok * n_smp * rows
     tok, smp = lax.axis_index("tok"), lax.axis_index("smp")
 
-    up_full = lax.all_gather(up_weight, "smp", axis=0, tiled=True)
     down_full = lax.all_gather(down_weight, "smp", axis=0, tiled=True)
 
     factor = jnp.exp((step_now[0] - last_step).astype(jnp.float32) * decay_log)
@@ -148,14 +232,27 @@
     looked = jnp.einsum(
         "gjcr,jrd->gjcd", pick.astype(jnp.float32), row_table * factor[:, :, None], precision=highest
     ).reshape(groups, rows, width)
-    lists = call(
-        functools.partial(lists_kernel, n_tok, n_smp),
-        looked,
-        (n_tok, n_smp, rows, width),
-        [],
-        [n_smp, n_smp, n_tok, n_tok],
-        1,
-    ).reshape(flat, width)
+    near = 2 if n_smp % 2 == 0 else 1
+    far = n_smp // near
+    up_blocks = up_weight.transpose(1, 0, 2)
+    hops = (local_toks, 2, far)
+    lists, up_full = pl.pallas_call(
+        functools.partial(lists_kernel, n_tok, n_smp, near),
+        out_shape=(
+            jax.ShapeDtypeStruct((n_tok, n_smp, rows, width), jnp.float32),
+            jax.ShapeDtypeStruct((local_toks, n_smp) + up_blocks.shape[1:], jnp.bfloat16),
+        ),
+        in_specs=[pl.BlockSpec(memory_space=VMEM)] * 2,
+        out_specs=(pl.BlockSpec(memory_space=VMEM),) * 2,
+        scratch_shapes=[pltpu.SemaphoreType.DMA((n,)) for n in (n_smp, n_smp, n_tok, n_tok)]
+        + [pltpu.SemaphoreType.DMA(n) for n in (hops, hops, (local_toks, far), (local_toks, far))],
+        compiler_params=pltpu.CompilerParams(
+            collective_id=1, has_side_effects=True, vmem_limit_bytes=24 << 20
+        ),
+        cost_estimate=pl.CostEstimate(flops=0, bytes_accessed=60_000_000, transcendentals=0),
+    )(looked, up_blocks)
+    lists = lists.reshape(flat, width)
+    up_full = up_full.reshape(local_toks, width, -1)
 
     place = jnp.arange(n_smp)[:, None] * capacity + jnp.arange(capacity)
     slots = sample_slots.reshape(n_tok, 1, local_toks, 1, batch)
@@ -173,7 +270,7 @@
     summed = jnp.einsum("kb,jkd->jbd", hits, jnp.stack(gathered), precision=highest)
     normed_in, inverse_in = normalize(summed)
     input_bf = normed_in.astype(jnp.bfloat16)
-    preact = jnp.einsum("jbd,djf->jbf", input_bf, up_full, preferred_element_type=jnp.float32)
+    preact = jnp.einsum("jbd,jdf->jbf", input_bf, up_full, preferred_element_type=jnp.float32)
     active = jax.nn.gelu(preact, approximate=False).astype(jnp.bfloat16)
     output = jnp.einsum("jbf,djf->jbd", active, down_full, preferred_element_type=jnp.float32)
     normed_out, inverse_out = normalize(normed_in + output)
@@ -190,37 +287,39 @@
     grad_sum = norm_back(dlogit[None, :, None] * out_weight[:, None, :], normed_out, inverse_out)
     grad_out_bf = grad_sum.astype(jnp.bfloat16)
 
-    near = 2 if n_smp % 2 == 0 else 1
-    far = n_smp // near
-    partial = jnp.einsum("jbd,jbf->jdf", grad_out_bf, active, preferred_element_type=jnp.float32)
-    partial = partial.reshape(local_toks, far, near, width // n_smp, -1)
     z, core = smp // near, smp % near
-    pair = lax.dynamic_index_in_dim(partial, core, 2, keepdims=False)
-    if near == 2:
-        other = lax.dynamic_index_in_dim(partial, 1 - core, 2, keepdims=False)
-        pair = pair + lax.ppermute(other, "smp", [(i, i ^ 1) for i in range(n_smp)])
+    pairs = []
+    for j in range(local_toks):
+        partial = jnp.einsum("bd,bf->df", grad_out_bf[j], active[j], preferred_element_type=jnp.float32)
+        partial = partial.reshape(far, near, width // n_smp, -1)
+        pair = lax.dynamic_index_in_dim(partial, core, 1, keepdims=False)
+        if near == 2:
+            other = lax.dynamic_index_in_dim(partial, 1 - core, 1, keepdims=False)
+            pair = pair + lax.ppermute(other, "smp", [(i, i ^ 1) for i in range(n_smp)])
+        pairs.append(pair)
+
     def far_sums(pair):
-        grad_down = lax.dynamic_index_in_dim(pair, z, 1, keepdims=False)
+        grad_down = lax.dynamic_index_in_dim(pair, z, 0, keepdims=False)
         flip = far & (far - 1) == 0
         for k in range(far - 1, 0, -1):
             partner = z ^ k if flip else (z + k) % far
-            part = lax.dynamic_index_in_dim(pair, partner, 1, keepdims=False)
+            part = lax.dynamic_index_in_dim(pair, partner, 0, keepdims=False)
             if not (flip and k == 1):
                 part = part.astype(jnp.bfloat16)
             route = [(i, i ^ (k * near) if flip else (i + k * near) % n_smp) for i in range(n_smp)]
             grad_down = grad_down + lax.ppermute(part, "smp", route).astype(jnp.float32)
-        return grad_down.transpose(1, 0, 2)
+        return grad_down
 
     grad_active = jnp.einsum(
         "jbd,djf->jbf", grad_out_bf, down_full, preferred_element_type=jnp.float32
     )
     grad_pre = (grad_active * gelu_grad(preact)).astype(jnp.bfloat16)
     grad_normed = grad_sum + jnp.einsum(
-        "jbf,djf->jbd", grad_pre, up_full, preferred_element_type=jnp.float32
+        "jbf,jdf->jbd", grad_pre, up_full, preferred_element_type=jnp.float32
     )
     grad_mixed = norm_back(grad_normed, normed_in, inverse_in)
-    pair, grad_mixed = lax.optimization_barrier((pair, grad_mixed))
-    grad_down = far_sums(pair)
+    pairs, grad_mixed = lax.optimization_barrier((pairs, grad_mixed))
+    grad_down = jnp.stack([far_sums(pair) for pair in pairs], axis=1)
 
     sums = jnp.einsum("kb,jbd->jkd", hits, grad_mixed, precision=highest)
     sent = jnp.zeros((flat, width), jnp.float32)

time: 148 us -> 149 us (level)
  waiting for transfers between devices: 36.3 us -> 6.98 us
  Pallas kernels: 43.4 us -> 68.3 us
  starting transfers between devices: 3.64 us -> 7.47 us
  other arithmetic: 18 us -> 19.9 us
    pallas_call x0 -> x1, Pallas kernels: none -> 47.1 us  [on_device(): pl.pallas_call(functools.partial(lists_kernel, n_tok, n_smp, near), out_s...]
    pallas_call x3 -> x2, Pallas kernels: 43.4 us -> 21.2 us  [call(): pl.pallas_call(kernel, out_shape=jax.ShapeDtypeStruct(out_shape, jnp.floa...]
    all_gather x1, waiting for transfers between devices: 20.5 us -> 0.01 us  [on_device(): down_full = lax.all_gather(down_weight, 'smp', axis=0, tiled=True)]
    all_gather x1 -> x0, waiting for transfers between devices: 15.8 us -> none  [on_device(): up_full = lax.all_gather(up_weight, 'smp', axis=0, tiled=True)]
    ppermute x3 -> x6, waiting for transfers between devices: 0.01 us -> 6.96 us  [far_sums(): grad_down = grad_down + lax.ppermute(part, 'smp', route).astype(jnp.float32)]
    dynamic_slice x2 -> x0, local copies, waits for them, and re-layouts: 5.15 us -> none  [the longest x1 3.25 us: on_device(): other = lax.dynamic_index_in_dim(partial, 1 - core, 2, keepdims=False)]
    ppermute x3 -> x6, starting transfers between devices: 3.55 us -> 6.97 us  [far_sums(): grad_down = grad_down + lax.ppermute(part, 'smp', route).astype(jnp.float32)]
    squeeze x1 -> x4, local copies, waits for them, and re-layouts: 0.05 us -> 3.27 us  [the longest x2 2.52 us: on_device(): other = lax.dynamic_index_in_dim(partial, 1 - core, 1, keepdims=False)]
  transfers between devices with their start and end apart: 6 -> 9, of which waited for: 2 -> 1; matrix products, arithmetic and copies ran while one was open for 19% -> 23% of each run, Pallas kernels for 26% -> 43%
where the time goes in v2:
time: 149 us; the launch traced here: 148 us
  Pallas kernels  68.3 us (46%)
  other arithmetic  19.9 us (13%)
  matrix products  15.4 us (10%)
  between operations  15.3 us (10%)
  local copies, waits for them, and re-layouts  14.8 us (10%)
  starting transfers between devices  7.47 us (5%)
  waiting for transfers between devices  6.98 us (5%)
    pallas_call x1, Pallas kernels, on_device(): pl.pallas_call(functools.partial(lists_kernel, n_tok, n_smp, near), out_s...  47.1 us
    pallas_call x2, Pallas kernels, call(): pl.pallas_call(kernel, out_shape=jax.ShapeDtypeStruct(out_shape, jnp.floa...  21.2 us
    convert_element_type x1, other arithmetic, on_device(): active = jax.nn.gelu(preact, approximate=False).astype(jnp.bfloat16)  7.94 us
    unnamed x34, local copies, waits for them, and re-layouts  7.32 us
    ppermute x6, starting transfers between devices, far_sums(): grad_down = grad_down + lax.ppermute(part, 'smp', route).astype(jnp.float32)  6.97 us
    ppermute x6, waiting for transfers between devices, far_sums(): grad_down = grad_down + lax.ppermute(part, 'smp', route).astype(jnp.float32)  6.96 us
    dot_general x1, matrix products, on_device(): jnp.einsum('jbf,jdf->jbd', grad_pre, up_full, preferred_element_type=jnp....  6.23 us
    dot_general x1, matrix products, on_device(): jnp.einsum('jbf,djf->jbd', active, down_full, preferred_element_type=jnp....  3.16 us
  transfers between devices with their start and end apart: 9, of which 1 were waited for; matrix products, arithmetic and copies ran while one was open for 23% of the time, Pallas kernels for 43%

profile of v2, /device:TPU:0, one launch (start us, length us, event | category | flops | bytes accessed | tf_op | source)
XLA Modules:
  0.0 148.2 jit_solution(882473999869369433)
XLA Ops:
  7.2 1.7 %copy.49 = bf16[48,2,1536]{2,0,1:T(8,128)(2,1)} copy(bf16[48,2,1536]{2,1,0:T(2,128)(2,1)} %param.20) | data formatting | bytes 589824 | tf_op args[9]
  9.6 0.7 multiply_exponential_fusion
  10.3 1.6 %fusion.19 = f32[2,384,8,2]{1,2,3,0:T(8,128)S(1)} fusion(f32[2,256,384]{2,1,0:T(8,128)} %param.11, f32[2,256]{1,0:T(2,128)S(1)} %multiply_exponential_fusion, s32[8,2,2]{0,2,1:T(2,128)} %bitcast.128), kind=kOutput, calls=%fused_computation.48 | convolution fusion | flops 37953536 | bytes 837760 | tf_op jit(solution)/shard_map/gjcr,jrd->gjcd/dot_general | solution.py:232
  12.0 1.0 copy.70
  13.0 47.1 %shard_map.138 = (f32[4,8,4,384]{3,2,1,0:T(4,128)S(1)}, bf16[2,8,48,1536]{3,2,1,0:T(8,128)(2,1)S(1)}) custom-call(f32[8,4,384]{2,1,0:T(4,128)S(1)} %copy.67.x_ref, bf16[2,48,1536]{2,1,0:T(8,128)(2,1)S(1)} %bitcast.116), custom_call_target="tpu_custom_call" | custom-call | bytes 60000000 | tf_op jit(solution)/shard_map/pallas_call | solution.py:239
  62.2 1.8 %fusion.22 = (u8[256,1536]{1,0:T(8,128)(4,1)S(1)}, u8[256,1536]{1,0:T(8,128)(4,1)S(1)}, f32[2,256,1536]{2,1,0:T(8,128)S(1)}) fusion(bf16[2,384,1536]{2,1,0:T(8,128)(2,1)S(1)} %bitcast.120, f32[2,256,384]{1,2,0:T(8,128)S(1)} %get-tuple-element.45, f32[2,256]{1,0:T(2,128)S(1)} %add_rsqrt_fusion.1, f32[2,256]{1,0:T(2,128)S(1)} %broadcast_multiply_fusion.5), kind=kOutput, calls=%fused_computation.58 | convolution fusion | flops 614006784 | bytes 7081984 | tf_op jit(solution)/shard_map/jbd,jdf->jbf/dot_general | solution.py:273
  64.1 1.7 %copy-done.8 = f32[2,256,1536]{2,1,0:T(8,128)} copy-done((f32[2,256,1536]{2,1,0:T(8,128)}, f32[2,256,1536]{2,1,0:T(8,128)S(1)}, u32[]{:S(2)}) %copy-start.8) | copy-done | bytes 3145752
  65.8 7.9 %fusion.2 = bf16[2,256,1536]{2,1,0:T(8,128)(2,1)} fusion(f32[2,256,1536]{2,1,0:T(8,128)S(1)} %get-tuple-element.46, u8[256,1536]{1,0:T(8,128)(4,1)S(1)} %get-tuple-element.23, u8[256,1536]{1,0:T(8,128)(4,1)S(1)} %get-tuple-element.22), kind=kLoop, calls=%fused_computation.5 | loop fusion | flops 55050240 | bytes 5505024 | tf_op jit(solution)/shard_map/convert_element_type | solution.py:274
  73.7 3.2 %fusion.82 = (f32[2,256]{1,0:T(2,128)S(1)}, f32[2,256,384]{1,2,0:T(8,128)S(1)}) fusion(bf16[2,256,1536]{2,1,0:T(8,128)(2,1)} %fusion.2, bf16[384,2,1536]{2,0,1:T(8,128)(2,1)} %all-gather.2.cloned.1.call-done, f32[2,256]{1,0:T(2,128)S(1)} %add_rsqrt_fusion.1, f32[2,256,384]{1,2,0:T(8,128)} %copy-done.5, f32[2,256]{1,0:T(2,128)S(1)} %broadcast_multiply_fusion.5), kind=kOutput, calls=%fused_computation.186 | convolution fusion | flops 604765696 | bytes 5511168 | tf_op jit(solution)/shard_map/jbf,djf->jbd/dot_general | solution.py:275
  77.2 4.7 %shard_map.139 = f32[1,256]{1,0:T(1,128)S(1)} custom-call(f32[1,256]{1,0:T(1,128)S(1)} %bitcast.119), custom_call_target="tpu_custom_call" | custom-call | bytes 30000000 | tf_op jit(solution)/shard_map/pallas_call | solution.py:187
  82.9 1.3 dynamic-slice_bitcast_fusion
  84.7 1.2 dynamic-slice_bitcast_fusion.1
  87.0 6.2 %fusion.78 = (f32[2,256]{1,0:T(2,128)S(1)}, f32[2,256]{1,0:T(2,128)S(1)}, f32[2,256,384]{1,2,0:T(8,128)}) fusion(f32[2,256]{1,0:T(2,128)S(1)} %add_rsqrt_fusion.1, f32[2,256,384]{1,2,0:T(8,128)} %copy-done.5, f32[2,256]{1,0:T(2,128)S(1)} %broadcast_multiply_fusion.5, bf16[2,384,1536]{2,1,0:T(8,128)(2,1)S(1)} %bitcast.121, f32[2,256,1536]{2,1,0:T(8,128)} %copy-done.8, ...), kind=kOutput, calls=%fused_computation.182 | convolution fusion | flops 1219951616 | bytes 10244096 | tf_op jit(solution)/shard_map/jbf,jdf->jbd/dot_general | solution.py:317
  93.2 1.7 %subtract_multiply_fusion = f32[2,256,384]{1,2,0:T(8,128)S(1)} fusion(f32[2,256,384]{1,2,0:T(8,128)} %get-tuple-element.49, f32[2,256,384]{1,2,0:T(8,128)} %copy-done.5, f32[2,256]{1,0:T(2,128)S(1)} %broadcast_multiply_fusion, f32[2,256]{1,0:T(2,128)S(1)} %broadcast_multiply_fusion.1, f32[2,256]{1,0:T(2,128)S(1)} %add_rsqrt_fusion.1, ...), kind=kLoop, calls=%fused_computation.52 | loop fusion | flops 1179648 | bytes 2367488 | tf_op jit(solution)/shard_map/mul | solution.py:28
  95.4 1.4 bitcast_add_fusion
  96.8 1.5 bitcast_add_fusion.1
  98.3 0.8 fusion.44
  99.1 1.7 %collective-permute-start.2 = (bf16[48,1536]{1,0:T(8,128)(2,1)}, bf16[48,1536]{1,0:T(8,128)(2,1)}, u32[]{:S(2)}, u32[]{:S(2)}) collective-permute-start(bf16[48,1536]{1,0:T(8,128)(2,1)} %get-tuple-element.32), channel_id=1, source_target_pairs={{0,6},{1,7},{2,4},{3,5},{4,2},{5,3},{6,0},{7,1},{8,14},{9,15},{10,... | collective-permute-start | bytes 442376 | tf_op jit(solution)/shard_map/ppermute | solution.py:310
  100.8 0.7 dynamic-slice_bitcast_fusion.3
  101.6 2.7 %collective-permute-start.4 = (f32[48,1536]{1,0:T(8,128)}, f32[48,1536]{1,0:T(8,128)}, u32[]{:S(2)}, u32[]{:S(2)}) collective-permute-start(f32[48,1536]{1,0:T(8,128)} %dynamic-slice_bitcast_fusion.3), channel_id=1, source_target_pairs={{0,2},{1,3},{2,0},{3,1},{4,6},{5,7},{6,4},{7,5},{8,10},{9,11},{10,... | collective-permute-start | bytes 884744 | tf_op jit(solution)/shard_map/ppermute | solution.py:310
  104.2 0.7 fusion.46
  105.0 1.7 %collective-permute-start.5 = (bf16[48,1536]{1,0:T(8,128)(2,1)}, bf16[48,1536]{1,0:T(8,128)(2,1)}, u32[]{:S(2)}, u32[]{:S(2)}) collective-permute-start(bf16[48,1536]{1,0:T(8,128)(2,1)} %get-tuple-element.34), channel_id=1, source_target_pairs={{0,6},{1,7},{2,4},{3,5},{4,2},{5,3},{6,0},{7,1},{8,14},{9,15},{10,... | collective-permute-start | bytes 442376 | tf_op jit(solution)/shard_map/ppermute | solution.py:310
  108.2 0.9 tile.43
  109.2 1.1 select_add_fusion.s_ref
  110.4 16.5 %shard_map.140 = f32[8,4,384]{2,1,0:T(4,128)S(1)} custom-call(f32[4,8,4,384]{3,2,1,0:T(4,128)S(1)} %select_add_fusion.s_ref), custom_call_target="tpu_custom_call" | custom-call | bytes 30000000 | tf_op jit(solution)/shard_map/pallas_call | solution.py:187
  126.9 0.7 multiply_reduce_fusion.1
  128.2 1.2 subtract_select_fusion.1
  129.4 0.9 collective-permute-start.7
  130.2 1.3 fusion.39
  131.5 6.9 %collective-permute-done.7 = f32[48,1536]{1,0:T(8,128)S(1)} collective-permute-done((f32[48,1536]{1,0:T(8,128)S(1)}, f32[48,1536]{1,0:T(8,128)S(1)}, u32[]{:S(2)}, u32[]{:S(2)}) %collective-permute-start.7) | collective-permute-done | bytes 294944 | tf_op jit(solution)/shard_map/ppermute | solution.py:310
  138.5 1.0 fusion.36
  139.5 1.3 copy.58
  (105 shorter events, 8.1 us)
Async XLA Ops:
  7.2 54.0 %copy-start.10 = (s32[2,1,8,2]{2,3,1,0:T(2,128)S(1)}, s32[2,1,8,2]{2,3,1,0:T(2,128)}, u32[]{:S(2)}) copy-start(s32[2,1,8,2]{2,3,1,0:T(2,128)} %param.15) | copy-start | bytes 388
  7.2 53.6 %copy-start.11 = (s32[8,256]{1,0:T(8,128)S(1)}, s32[8,256]{1,0:T(8,128)}, u32[]{:S(2)}) copy-start(s32[8,256]{1,0:T(8,128)} %param.17) | copy-start | bytes 24580
  7.2 54.0 %copy-start.14 = (s32[2,1,8]{2,1,0:T(1,128)S(1)}, s32[2,1,8]{2,1,0:T(1,128)}, u32[]{:S(2)}) copy-start(s32[2,1,8]{2,1,0:T(1,128)} %param.16) | copy-start | bytes 196
  7.2 66.5 %all-gather.2.cloned.1.call-start = ((), (), s32[]{:S(2)}) async-start(), calls=%async_computation | async-start | bytes 2654208 | tf_op jit(solution)/shard_map/all_gather | solution.py:226
  62.0 2.1 %copy-start.5 = (f32[2,256,384]{1,2,0:T(8,128)}, f32[2,256,384]{1,2,0:T(8,128)S(1)}, u32[]{:S(2)}) copy-start(f32[2,256,384]{1,2,0:T(8,128)S(1)} %get-tuple-element.45) | copy-start | bytes 2359300
  64.1 1.7 %copy-start.8 = (f32[2,256,1536]{2,1,0:T(8,128)}, f32[2,256,1536]{2,1,0:T(8,128)S(1)}, u32[]{:S(2)}) copy-start(f32[2,256,1536]{2,1,0:T(8,128)S(1)} %get-tuple-element.46) | copy-start | bytes 9437188
  73.7 3.3 %copy-start.9 = (f32[2,384]{1,0:T(2,128)S(1)}, f32[2,384]{1,0:T(2,128)}, u32[]{:S(2)}) copy-start(f32[2,384]{1,0:T(2,128)} %param.21) | copy-start | bytes 9220
  73.7 8.2 %copy-start.13 = (s32[256]{0:T(256)S(1)}, s32[256]{0:T(256)}, u32[]{:S(2)}) copy-start(s32[256]{0:T(256)} %param.18) | copy-start | bytes 3076
  76.9 5.5 %copy-start.4 = (bf16[2,256,1536]{2,1,0:T(8,128)(2,1)S(1)}, bf16[2,256,1536]{2,1,0:T(8,128)(2,1)}, u32[]{:S(2)}) copy-start(bf16[2,256,1536]{2,1,0:T(8,128)(2,1)} %fusion.2) | copy-start | bytes 4718596
  82.9 1.8 %copy-start = (f32[4,2,48,1536]{3,2,1,0:T(8,128)}, f32[4,2,48,1536]{3,2,1,0:T(8,128)S(1)}, u32[]{:S(2)}) copy-start(f32[4,2,48,1536]{3,2,1,0:T(8,128)S(1)} %fusion.17) | copy-start | bytes 7077892
  84.2 10.7 %collective-permute-start.1 = (f32[4,48,1536]{2,1,0:T(8,128)}, f32[4,48,1536]{2,1,0:T(8,128)}, u32[]{:S(2)}, u32[]{:S(2)}) collective-permute-start(f32[4,48,1536]{2,1,0:T(8,128)} %dynamic-slice_bitcast_fusion), channel_id=1, source_target_pairs={{0,1},{1,0},{2,3},{3,2},{4,5},{5,4},{6,7},{7,6},{8,9},{9,8},{10,11... | collective-permute-start | bytes 3538952 | tf_op jit(solution)/shard_map/ppermute | solution.py:298
  84.7 1.8 %copy-start.2 = (f32[4,2,48,1536]{3,2,1,0:T(8,128)}, f32[4,2,48,1536]{3,2,1,0:T(8,128)S(1)}, u32[]{:S(2)}) copy-start(f32[4,2,48,1536]{3,2,1,0:T(8,128)S(1)} %fusion.18) | copy-start | bytes 7077892
  86.5 10.3 %collective-permute-start = (f32[4,48,1536]{2,1,0:T(8,128)}, f32[4,48,1536]{2,1,0:T(8,128)}, u32[]{:S(2)}, u32[]{:S(2)}) collective-permute-start(f32[4,48,1536]{2,1,0:T(8,128)} %dynamic-slice_bitcast_fusion.1), channel_id=1, source_target_pairs={{0,1},{1,0},{2,3},{3,2},{4,5},{5,4},{6,7},{7,6},{8,9},{9,8},{10,11... | collective-permute-start | bytes 3538952 | tf_op jit(solution)/shard_map/ppermute | solution.py:298
  93.2 2.1 %copy-start.1 = (f32[4,2,48,1536]{3,2,1,0:T(8,128)S(1)}, f32[4,2,48,1536]{3,2,1,0:T(8,128)}, u32[]{:S(2)}) copy-start(f32[4,2,48,1536]{3,2,1,0:T(8,128)} %copy-done) | copy-start | bytes 7077892
  93.2 3.6 %copy-start.3 = (f32[4,2,48,1536]{3,2,1,0:T(8,128)S(1)}, f32[4,2,48,1536]{3,2,1,0:T(8,128)}, u32[]{:S(2)}) copy-start(f32[4,2,48,1536]{3,2,1,0:T(8,128)} %copy-done.2) | copy-start | bytes 7077892
  98.3 2.6 %copy-start.6 = (f32[4,48,1536]{2,1,0:T(8,128)}, f32[4,48,1536]{2,1,0:T(8,128)S(1)}, u32[]{:S(2)}) copy-start(f32[4,48,1536]{2,1,0:T(8,128)S(1)} %bitcast_add_fusion.1) | copy-start | bytes 3538948
  99.1 30.3 %collective-permute-start.2 = (bf16[48,1536]{1,0:T(8,128)(2,1)}, bf16[48,1536]{1,0:T(8,128)(2,1)}, u32[]{:S(2)}, u32[]{:S(2)}) collective-permute-start(bf16[48,1536]{1,0:T(8,128)(2,1)} %get-tuple-element.32), channel_id=1, source_target_pairs={{0,6},{1,7},{2,4},{3,5},{4,2},{5,3},{6,0},{7,1},{8,14},{9,15},{10,... | collective-permute-start | bytes 442376 | tf_op jit(solution)/shard_map/ppermute | solution.py:310
  100.8 29.4 %collective-permute-start.3 = (bf16[48,1536]{1,0:T(8,128)(2,1)}, bf16[48,1536]{1,0:T(8,128)(2,1)}, u32[]{:S(2)}, u32[]{:S(2)}) collective-permute-start(bf16[48,1536]{1,0:T(8,128)(2,1)} %get-tuple-element.33), channel_id=1, source_target_pairs={{0,4},{1,5},{2,6},{3,7},{4,0},{5,1},{6,2},{7,3},{8,12},{9,13},{10,... | collective-permute-start | bytes 442376 | tf_op jit(solution)/shard_map/ppermute | solution.py:310
  101.6 28.7 %collective-permute-start.4 = (f32[48,1536]{1,0:T(8,128)}, f32[48,1536]{1,0:T(8,128)}, u32[]{:S(2)}, u32[]{:S(2)}) collective-permute-start(f32[48,1536]{1,0:T(8,128)} %dynamic-slice_bitcast_fusion.3), channel_id=1, source_target_pairs={{0,2},{1,3},{2,0},{3,1},{4,6},{5,7},{6,4},{7,5},{8,10},{9,11},{10,... | collective-permute-start | bytes 884744 | tf_op jit(solution)/shard_map/ppermute | solution.py:310
  105.0 26.5 %collective-permute-start.5 = (bf16[48,1536]{1,0:T(8,128)(2,1)}, bf16[48,1536]{1,0:T(8,128)(2,1)}, u32[]{:S(2)}, u32[]{:S(2)}) collective-permute-start(bf16[48,1536]{1,0:T(8,128)(2,1)} %get-tuple-element.34), channel_id=1, source_target_pairs={{0,6},{1,7},{2,4},{3,5},{4,2},{5,3},{6,0},{7,1},{8,14},{9,15},{10,... | collective-permute-start | bytes 442376 | tf_op jit(solution)/shard_map/ppermute | solution.py:310
  106.7 24.8 %collective-permute-start.6 = (bf16[48,1536]{1,0:T(8,128)(2,1)}, bf16[48,1536]{1,0:T(8,128)(2,1)}, u32[]{:S(2)}, u32[]{:S(2)}) collective-permute-start(bf16[48,1536]{1,0:T(8,128)(2,1)} %get-tuple-element.35), channel_id=1, source_target_pairs={{0,4},{1,5},{2,6},{3,7},{4,0},{5,1},{6,2},{7,3},{8,12},{9,13},{10,... | collective-permute-start | bytes 442376 | tf_op jit(solution)/shard_map/ppermute | solution.py:310
  107.5 20.1 %copy-start.12 = (f32[2,256]{1,0:T(2,128)S(1)}, f32[2,256]{1,0:T(2,128)}, u32[]{:S(2)}) copy-start(f32[2,256]{1,0:T(2,128)} %param.12) | copy-start | bytes 6148
  107.5 20.7 %copy-start.7 = (f32[2,256,384]{2,1,0:T(8,128)S(1)}, f32[2,256,384]{2,1,0:T(8,128)}, u32[]{:S(2)}) copy-start(f32[2,256,384]{2,1,0:T(8,128)} %param.11) | copy-start | bytes 2359300
  129.4 9.1 %collective-permute-start.7 = (f32[48,1536]{1,0:T(8,128)S(1)}, f32[48,1536]{1,0:T(8,128)S(1)}, u32[]{:S(2)}, u32[]{:S(2)}) collective-permute-start(f32[48,1536]{1,0:T(8,128)S(1)} %dynamic-slice_bitcast_fusion.2), channel_id=1, source_target_pairs={{0,2},{1,3},{2,0},{3,1},{4,6},{5,7},{6,4},{7,5},{8,10},{9,11},{10,... | collective-permute-start | bytes 884744 | tf_op jit(solution)/shard_map/ppermute | solution.py:310
Sparse Core Ops, SparseCore 0:
  10.2 43.4 all-gather.1

commit v3 on v2

--- a/solution.py
+++ b/solution.py
@@ -222,8 +222,6 @@
     rows = local_toks * capacity
     flat = n_tok * n_smp * rows
     tok, smp = lax.axis_index("tok"), lax.axis_index("smp")
-
-    down_full = lax.all_gather(down_weight, "smp", axis=0, tiled=True)
 
     factor = jnp.exp((step_now[0] - last_step).astype(jnp.float32) * decay_log)
     ids = row_ids[:, 0].transpose(1, 0, 2)
@@ -251,6 +249,8 @@
         ),
         cost_estimate=pl.CostEstimate(flops=0, bytes_accessed=60_000_000, transcendentals=0),
     )(looked, up_blocks)
+    lists, up_full, down_weight = lax.optimization_barrier((lists, up_full, down_weight))
+    down_full = lax.all_gather(down_weight, "smp", axis=0, tiled=True)
     lists = lists.reshape(flat, width)
     up_full = up_full.reshape(local_toks, width, -1)
 
@@ -298,17 +298,20 @@
             pair = pair + lax.ppermute(other, "smp", [(i, i ^ 1) for i in range(n_smp)])
         pairs.append(pair)
 
-    def far_sums(pair):
-        grad_down = lax.dynamic_index_in_dim(pair, z, 0, keepdims=False)
+    def far_sums(pairs):
+        def blocks(position):
+            parts = [lax.dynamic_index_in_dim(pair, position, 0, keepdims=False) for pair in pairs]
+            return jnp.concatenate(parts, axis=0)
+
+        grad_down = blocks(z)
         flip = far & (far - 1) == 0
         for k in range(far - 1, 0, -1):
-            partner = z ^ k if flip else (z + k) % far
-            part = lax.dynamic_index_in_dim(pair, partner, 0, keepdims=False)
+            part = blocks(z ^ k if flip else (z + k) % far)
             if not (flip and k == 1):
                 part = part.astype(jnp.bfloat16)
             route = [(i, i ^ (k * near) if flip else (i + k * near) % n_smp) for i in range(n_smp)]
             grad_down = grad_down + lax.ppermute(part, "smp", route).astype(jnp.float32)
-        return grad_down
+        return jnp.stack(jnp.split(grad_down, local_toks, axis=0), axis=1)
 
     grad_active = jnp.einsum(
         "jbd,djf->jbf", grad_out_bf, down_full, preferred_element_type=jnp.float32
@@ -319,7 +322,7 @@
     )
     grad_mixed = norm_back(grad_normed, normed_in, inverse_in)
     pairs, grad_mixed = lax.optimization_barrier((pairs, grad_mixed))
-    grad_down = jnp.stack([far_sums(pair) for pair in pairs], axis=1)
+    grad_down = far_sums(pairs)
 
     sums = jnp.einsum("kb,jbd->jkd", hits, grad_mixed, precision=highest)
     sent = jnp.zeros((flat, width), jnp.float32)

time: 149 us -> 141 us (0.946)
  Pallas kernels: 68.3 us -> 55.7 us
  waiting for transfers between devices: 6.98 us -> 17.3 us
  local copies, waits for them, and re-layouts: 14.8 us -> 12.1 us
  starting transfers between devices: 7.47 us -> 4.88 us
    pallas_call x1, Pallas kernels: 47.1 us -> 28.1 us  [on_device(): pl.pallas_call(functools.partial(lists_kernel, n_tok, n_smp, near), out_s...]
    all_gather x1, waiting for transfers between devices: 0.01 us -> 17.3 us  [on_device(): down_full = lax.all_gather(down_weight, 'smp', axis=0, tiled=True)]
    ppermute x6 -> x3, waiting for transfers between devices: 6.96 us -> 0.01 us  [far_sums(): grad_down = grad_down + lax.ppermute(part, 'smp', route).astype(jnp.float32)]
    pallas_call x2, Pallas kernels: 21.2 us -> 27.6 us  [call(): pl.pallas_call(kernel, out_shape=jax.ShapeDtypeStruct(out_shape, jnp.floa...]
    ppermute x6 -> x3, starting transfers between devices: 6.97 us -> 4.39 us  [far_sums(): grad_down = grad_down + lax.ppermute(part, 'smp', route).astype(jnp.float32)]
    concatenate x0 -> x3, other arithmetic: none -> 2.32 us  [blocks(): return jnp.concatenate(parts, axis=0)]
    another operation x3 -> x1, other arithmetic: 2.33 us -> 0.04 us  [far_sums(): return jnp.stack(jnp.split(grad_down, local_toks, axis=0), axis=1)]
    unnamed x34 -> x31, local copies, waits for them, and re-layouts: 7.32 us -> 5.61 us
  transfers between devices with their start and end apart: 9 -> 6, of which waited for: 1 -> 1; matrix products, arithmetic and copies ran while one was open for 23% -> 20% of each run, Pallas kernels for 43% -> 16%
where the time goes in v3:
time: 141 us
  Pallas kernels  55.7 us (40%)
  other arithmetic  20.3 us (14%)
  waiting for transfers between devices  17.3 us (12%)
  matrix products  15.4 us (11%)
  between operations  15.3 us (11%)
  local copies, waits for them, and re-layouts  12.1 us (9%)
  starting transfers between devices  4.88 us (3%)
    pallas_call x1, Pallas kernels, on_device(): pl.pallas_call(functools.partial(lists_kernel, n_tok, n_smp, near), out_s...  28.1 us
    pallas_call x2, Pallas kernels, call(): pl.pallas_call(kernel, out_shape=jax.ShapeDtypeStruct(out_shape, jnp.floa...  27.6 us
    all_gather x1, waiting for transfers between devices, on_device(): down_full = lax.all_gather(down_weight, 'smp', axis=0, tiled=True)  17.3 us
    convert_element_type x1, other arithmetic, on_device(): active = jax.nn.gelu(preact, approximate=False).astype(jnp.bfloat16)  7.94 us
    dot_general x1, matrix products, on_device(): jnp.einsum('jbf,jdf->jbd', grad_pre, up_full, preferred_element_type=jnp....  6.23 us
    unnamed x31, local copies, waits for them, and re-layouts  5.61 us
    ppermute x3, starting transfers between devices, far_sums(): grad_down = grad_down + lax.ppermute(part, 'smp', route).astype(jnp.float32)  4.39 us
    dot_general x1, matrix products, on_device(): jnp.einsum('jbf,djf->jbd', active, down_full, preferred_element_type=jnp....  3.14 us
  transfers between devices with their start and end apart: 6, of which 1 were waited for; matrix products, arithmetic and copies ran while one was open for 20% of the time, Pallas kernels for 16%

profile of v3, /device:TPU:0, one launch (start us, length us, event | category | flops | bytes accessed | tf_op | source)
XLA Modules:
  0.0 141.0 jit_solution(6438845302455063753)
XLA Ops:
  7.9 0.7 multiply_exponential_fusion
  8.6 1.6 %fusion.19 = f32[2,384,8,2]{1,2,3,0:T(8,128)S(1)} fusion(f32[2,256,384]{2,1,0:T(8,128)} %param.11, f32[2,256]{1,0:T(2,128)S(1)} %multiply_exponential_fusion, s32[8,2,2]{0,2,1:T(2,128)} %bitcast.116), kind=kOutput, calls=%fused_computation.48 | convolution fusion | flops 37953536 | bytes 837760 | tf_op jit(solution)/shard_map/gjcr,jrd->gjcd/dot_general | solution.py:230
  10.2 1.0 copy.71
  11.2 28.1 %shard_map.138 = (f32[4,8,4,384]{3,2,1,0:T(4,128)S(1)}, bf16[2,8,48,1536]{3,2,1,0:T(8,128)(2,1)S(1)}) custom-call(f32[8,4,384]{2,1,0:T(4,128)S(1)} %copy.68.x_ref, bf16[2,48,1536]{2,1,0:T(8,128)(2,1)S(1)} %bitcast.104), custom_call_target="tpu_custom_call" | custom-call | bytes 60000000 | tf_op jit(solution)/shard_map/pallas_call | solution.py:237
  39.3 1.7 %copy.50 = bf16[48,2,1536]{2,0,1:T(8,128)(2,1)} copy(bf16[48,2,1536]{2,1,0:T(2,128)(2,1)} %param.20) | data formatting | bytes 589824 | tf_op jit(solution)/shard_map/optimization_barrier | solution.py:252
  43.3 1.8 %fusion.22 = (u8[256,1536]{1,0:T(8,128)(4,1)S(1)}, u8[256,1536]{1,0:T(8,128)(4,1)S(1)}, f32[2,256,1536]{2,1,0:T(8,128)S(1)}) fusion(bf16[2,384,1536]{2,1,0:T(8,128)(2,1)S(1)} %bitcast.108, f32[2,256,384]{1,2,0:T(8,128)S(1)} %get-tuple-element.57, f32[2,256]{1,0:T(2,128)S(1)} %add_rsqrt_fusion.1, f32[2,256]{1,0:T(2,128)S(1)} %broadcast_multiply_fusion.5), kind=kOutput, calls=%fused_computation.58 | convolution fusion | flops 614006784 | bytes 7081984 | tf_op jit(solution)/shard_map/jbd,jdf->jbf/dot_general | solution.py:273
  45.1 1.7 %copy-done.7 = f32[2,256,1536]{2,1,0:T(8,128)} copy-done((f32[2,256,1536]{2,1,0:T(8,128)}, f32[2,256,1536]{2,1,0:T(8,128)S(1)}, u32[]{:S(2)}) %copy-start.7) | copy-done | bytes 3145752
  46.8 7.9 %fusion.2 = bf16[2,256,1536]{2,1,0:T(8,128)(2,1)} fusion(f32[2,256,1536]{2,1,0:T(8,128)S(1)} %get-tuple-element.58, u8[256,1536]{1,0:T(8,128)(4,1)S(1)} %get-tuple-element.29, u8[256,1536]{1,0:T(8,128)(4,1)S(1)} %get-tuple-element.28), kind=kLoop, calls=%fused_computation.5 | loop fusion | flops 55050240 | bytes 5505024 | tf_op jit(solution)/shard_map/convert_element_type | solution.py:274
  54.7 17.3 %all-gather.2.cloned.1.call-done = bf16[384,2,1536]{2,0,1:T(8,128)(2,1)} async-done(((bf16[48,2,1536]{2,0,1:T(8,128)(2,1)}), bf16[384,2,1536]{2,0,1:T(8,128)(2,1)}) %all-gather.2.cloned.1.call-update) | async-done | bytes 2359312 | tf_op jit(solution)/shard_map/all_gather | solution.py:253
  72.0 3.1 %fusion.78 = (f32[2,256]{1,0:T(2,128)S(1)}, f32[2,256,384]{1,2,0:T(8,128)S(1)}) fusion(bf16[2,256,1536]{2,1,0:T(8,128)(2,1)} %fusion.2, bf16[384,2,1536]{2,0,1:T(8,128)(2,1)} %all-gather.2.cloned.1.call-done, f32[2,256]{1,0:T(2,128)S(1)} %add_rsqrt_fusion.1, f32[2,256,384]{1,2,0:T(8,128)} %copy-done.5, f32[2,256]{1,0:T(2,128)S(1)} %broadcast_multiply_fusion.5), kind=kOutput, calls=%fused_computation.188 | convolution fusion | flops 604765696 | bytes 5511168 | tf_op jit(solution)/shard_map/jbf,djf->jbd/dot_general | solution.py:275
  75.5 4.6 %shard_map.139 = f32[1,256]{1,0:T(1,128)S(1)} custom-call(f32[1,256]{1,0:T(1,128)S(1)} %bitcast.107), custom_call_target="tpu_custom_call" | custom-call | bytes 30000000 | tf_op jit(solution)/shard_map/pallas_call | solution.py:187
  81.1 1.3 dynamic-slice_bitcast_fusion
  83.0 1.2 dynamic-slice_bitcast_fusion.1
  84.2 0.6 copy-done.2
  85.2 6.2 %fusion.74 = (f32[2,256]{1,0:T(2,128)S(1)}, f32[2,256]{1,0:T(2,128)S(1)}, f32[2,256,384]{1,2,0:T(8,128)}) fusion(f32[2,256]{1,0:T(2,128)S(1)} %add_rsqrt_fusion.1, f32[2,256,384]{1,2,0:T(8,128)} %copy-done.5, f32[2,256]{1,0:T(2,128)S(1)} %broadcast_multiply_fusion.5, bf16[2,384,1536]{2,1,0:T(8,128)(2,1)S(1)} %bitcast.109, f32[2,256,1536]{2,1,0:T(8,128)} %copy-done.7, ...), kind=kOutput, calls=%fused_computation.184 | convolution fusion | flops 1219951616 | bytes 10244096 | tf_op jit(solution)/shard_map/jbf,jdf->jbd/dot_general | solution.py:320
  91.5 1.7 %subtract_multiply_fusion = f32[2,256,384]{1,2,0:T(8,128)S(1)} fusion(f32[2,256,384]{1,2,0:T(8,128)} %get-tuple-element.61, f32[2,256,384]{1,2,0:T(8,128)} %copy-done.5, f32[2,256]{1,0:T(2,128)S(1)} %broadcast_multiply_fusion, f32[2,256]{1,0:T(2,128)S(1)} %broadcast_multiply_fusion.1, f32[2,256]{1,0:T(2,128)S(1)} %add_rsqrt_fusion.1, ...), kind=kLoop, calls=%fused_computation.52 | loop fusion | flops 1179648 | bytes 2367488 | tf_op jit(solution)/shard_map/mul | solution.py:28
  93.6 1.4 %bitcast_add_fusion = f32[4,48,1536]{2,1,0:T(8,128)S(1)} fusion(f32[4,48,1536]{2,1,0:T(8,128)} %collective-permute-done.1, f32[4,2,48,1536]{3,2,1,0:T(8,128)S(1)} %copy-done.1, s32[]{:T(128)S(6)} %select_n.254), kind=kLoop, calls=%fused_computation.37 | loop fusion | flops 294912 | bytes 3538948 | tf_op jit(solution)/shard_map/add | solution.py:298
  95.1 1.5 %bitcast_add_fusion.1 = f32[4,48,1536]{2,1,0:T(8,128)S(1)} fusion(f32[4,48,1536]{2,1,0:T(8,128)} %collective-permute-done, f32[4,2,48,1536]{3,2,1,0:T(8,128)S(1)} %copy-done.3, s32[]{:T(128)S(6)} %select_n.254), kind=kLoop, calls=%fused_computation.38 | loop fusion | flops 294912 | bytes 3538948 | tf_op jit(solution)/shard_map/add | solution.py:298
  96.7 0.7 pad_maximum_fusion.2
  97.5 1.5 %collective-permute-start.2 = (bf16[96,1536]{1,0:T(8,128)(2,1)}, bf16[96,1536]{1,0:T(8,128)(2,1)S(1)}, u32[]{:S(2)}, u32[]{:S(2)}) collective-permute-start(bf16[96,1536]{1,0:T(8,128)(2,1)} %pad_maximum_fusion.2), channel_id=1, source_target_pairs={{0,6},{1,7},{2,4},{3,5},{4,2},{5,3},{6,0},{7,1},{8,14},{9,15},{10,... | collective-permute-start | bytes 884744 | tf_op jit(solution)/shard_map/ppermute | solution.py:313
  99.0 0.7 pad_maximum_fusion.3
  99.7 0.9 collective-permute-start.3
  100.7 0.9 pad_maximum_fusion
  101.5 1.9 %collective-permute-start.4 = (f32[96,1536]{1,0:T(8,128)}, f32[96,1536]{1,0:T(8,128)}, u32[]{:S(2)}, u32[]{:S(2)}) collective-permute-start(f32[96,1536]{1,0:T(8,128)} %pad_maximum_fusion), channel_id=1, source_target_pairs={{0,2},{1,3},{2,0},{3,1},{4,6},{5,7},{6,4},{7,5},{8,10},{9,11},{10,... | collective-permute-start | bytes 1769480 | tf_op jit(solution)/shard_map/ppermute | solution.py:313
  103.4 0.5 convolution_bitcast_fusion.2
  105.5 23.0 %shard_map.140 = f32[8,4,384]{2,1,0:T(4,128)S(1)} custom-call(f32[4,8,4,384]{3,2,1,0:T(4,128)S(1)} %select_add_fusion.s_ref), custom_call_target="tpu_custom_call" | custom-call | bytes 30000000 | tf_op jit(solution)/shard_map/pallas_call | solution.py:187
  128.5 0.7 multiply_reduce_fusion.1
  129.1 0.6 rsqrt_multiply_fusion
  129.7 1.2 subtract_select_fusion.1
  130.9 1.3 fusion.25
  132.3 1.3 copy.59
  133.6 0.6 copy.77
  (100 shorter events, 6.4 us)
Async XLA Ops:
  7.2 35.0 %copy-start.9 = (s32[2,1,8,2]{2,3,1,0:T(2,128)S(1)}, s32[2,1,8,2]{2,3,1,0:T(2,128)}, u32[]{:S(2)}) copy-start(s32[2,1,8,2]{2,3,1,0:T(2,128)} %param.15) | copy-start | bytes 388
  7.2 34.6 %copy-start.10 = (s32[8,256]{1,0:T(8,128)S(1)}, s32[8,256]{1,0:T(8,128)}, u32[]{:S(2)}) copy-start(s32[8,256]{1,0:T(8,128)} %param.17) | copy-start | bytes 24580
  7.2 35.0 %copy-start.13 = (s32[2,1,8]{2,1,0:T(1,128)S(1)}, s32[2,1,8]{2,1,0:T(1,128)}, u32[]{:S(2)}) copy-start(s32[2,1,8]{2,1,0:T(1,128)} %param.16) | copy-start | bytes 196
  7.2 64.8 %all-gather.2.cloned.1.call-start = ((), (), s32[]{:S(2)}) async-start(), calls=%async_computation | async-start | bytes 2654208 | tf_op jit(solution)/shard_map/all_gather | solution.py:253
  43.0 2.1 %copy-start.5 = (f32[2,256,384]{1,2,0:T(8,128)}, f32[2,256,384]{1,2,0:T(8,128)S(1)}, u32[]{:S(2)}) copy-start(f32[2,256,384]{1,2,0:T(8,128)S(1)} %get-tuple-element.57) | copy-start | bytes 2359300
  45.1 1.7 %copy-start.7 = (f32[2,256,1536]{2,1,0:T(8,128)}, f32[2,256,1536]{2,1,0:T(8,128)S(1)}, u32[]{:S(2)}) copy-start(f32[2,256,1536]{2,1,0:T(8,128)S(1)} %get-tuple-element.58) | copy-start | bytes 9437188
  54.7 20.6 %copy-start.8 = (f32[2,384]{1,0:T(2,128)S(1)}, f32[2,384]{1,0:T(2,128)}, u32[]{:S(2)}) copy-start(f32[2,384]{1,0:T(2,128)} %param.21) | copy-start | bytes 9220
  54.7 25.4 %copy-start.12 = (s32[256]{0:T(256)S(1)}, s32[256]{0:T(256)}, u32[]{:S(2)}) copy-start(s32[256]{0:T(256)} %param.18) | copy-start | bytes 3076
  75.1 5.5 %copy-start.4 = (bf16[2,256,1536]{2,1,0:T(8,128)(2,1)S(1)}, bf16[2,256,1536]{2,1,0:T(8,128)(2,1)}, u32[]{:S(2)}) copy-start(bf16[2,256,1536]{2,1,0:T(8,128)(2,1)} %fusion.2) | copy-start | bytes 4718596
  81.1 1.8 %copy-start = (f32[4,2,48,1536]{3,2,1,0:T(8,128)}, f32[4,2,48,1536]{3,2,1,0:T(8,128)S(1)}, u32[]{:S(2)}) copy-start(f32[4,2,48,1536]{3,2,1,0:T(8,128)S(1)} %fusion.17) | copy-start | bytes 7077892
  82.4 10.7 %collective-permute-start.1 = (f32[4,48,1536]{2,1,0:T(8,128)}, f32[4,48,1536]{2,1,0:T(8,128)}, u32[]{:S(2)}, u32[]{:S(2)}) collective-permute-start(f32[4,48,1536]{2,1,0:T(8,128)} %dynamic-slice_bitcast_fusion), channel_id=1, source_target_pairs={{0,1},{1,0},{2,3},{3,2},{4,5},{5,4},{6,7},{7,6},{8,9},{9,8},{10,11... | collective-permute-start | bytes 3538952 | tf_op jit(solution)/shard_map/ppermute | solution.py:298
  83.0 1.8 %copy-start.2 = (f32[4,2,48,1536]{3,2,1,0:T(8,128)}, f32[4,2,48,1536]{3,2,1,0:T(8,128)S(1)}, u32[]{:S(2)}) copy-start(f32[4,2,48,1536]{3,2,1,0:T(8,128)S(1)} %fusion.18) | copy-start | bytes 7077892
  84.8 10.3 %collective-permute-start = (f32[4,48,1536]{2,1,0:T(8,128)}, f32[4,48,1536]{2,1,0:T(8,128)}, u32[]{:S(2)}, u32[]{:S(2)}) collective-permute-start(f32[4,48,1536]{2,1,0:T(8,128)} %dynamic-slice_bitcast_fusion.1), channel_id=1, source_target_pairs={{0,1},{1,0},{2,3},{3,2},{4,5},{5,4},{6,7},{7,6},{8,9},{9,8},{10,11... | collective-permute-start | bytes 3538952 | tf_op jit(solution)/shard_map/ppermute | solution.py:298
  91.5 2.1 %copy-start.1 = (f32[4,2,48,1536]{3,2,1,0:T(8,128)S(1)}, f32[4,2,48,1536]{3,2,1,0:T(8,128)}, u32[]{:S(2)}) copy-start(f32[4,2,48,1536]{3,2,1,0:T(8,128)} %copy-done) | copy-start | bytes 7077892
  91.5 3.6 %copy-start.3 = (f32[4,2,48,1536]{3,2,1,0:T(8,128)S(1)}, f32[4,2,48,1536]{3,2,1,0:T(8,128)}, u32[]{:S(2)}) copy-start(f32[4,2,48,1536]{3,2,1,0:T(8,128)} %copy-done.2) | copy-start | bytes 7077892
  97.5 33.4 %collective-permute-start.2 = (bf16[96,1536]{1,0:T(8,128)(2,1)}, bf16[96,1536]{1,0:T(8,128)(2,1)S(1)}, u32[]{:S(2)}, u32[]{:S(2)}) collective-permute-start(bf16[96,1536]{1,0:T(8,128)(2,1)} %pad_maximum_fusion.2), channel_id=1, source_target_pairs={{0,6},{1,7},{2,4},{3,5},{4,2},{5,3},{6,0},{7,1},{8,14},{9,15},{10,... | collective-permute-start | bytes 884744 | tf_op jit(solution)/shard_map/ppermute | solution.py:313
  99.7 31.2 %collective-permute-start.3 = (bf16[96,1536]{1,0:T(8,128)(2,1)}, bf16[96,1536]{1,0:T(8,128)(2,1)}, u32[]{:S(2)}, u32[]{:S(2)}) collective-permute-start(bf16[96,1536]{1,0:T(8,128)(2,1)} %pad_maximum_fusion.3), channel_id=1, source_target_pairs={{0,4},{1,5},{2,6},{3,7},{4,0},{5,1},{6,2},{7,3},{8,12},{9,13},{10,... | collective-permute-start | bytes 884744 | tf_op jit(solution)/shard_map/ppermute | solution.py:313
  101.5 29.4 %collective-permute-start.4 = (f32[96,1536]{1,0:T(8,128)}, f32[96,1536]{1,0:T(8,128)}, u32[]{:S(2)}, u32[]{:S(2)}) collective-permute-start(f32[96,1536]{1,0:T(8,128)} %pad_maximum_fusion), channel_id=1, source_target_pairs={{0,2},{1,3},{2,0},{3,1},{4,6},{5,7},{6,4},{7,5},{8,10},{9,11},{10,... | collective-permute-start | bytes 1769480 | tf_op jit(solution)/shard_map/ppermute | solution.py:313
  104.2 24.9 %copy-start.11 = (f32[2,256]{1,0:T(2,128)S(1)}, f32[2,256]{1,0:T(2,128)}, u32[]{:S(2)}) copy-start(f32[2,256]{1,0:T(2,128)} %param.12) | copy-start | bytes 6148
  104.3 25.5 %copy-start.6 = (f32[2,256,384]{2,1,0:T(8,128)S(1)}, f32[2,256,384]{2,1,0:T(8,128)}, u32[]{:S(2)}) copy-start(f32[2,256,384]{2,1,0:T(8,128)} %param.11) | copy-start | bytes 2359300
Sparse Core Ops, SparseCore 0:
  41.2 30.7 all-gather.1
